TPU v7x, 128 devices: a whole 4x4x4 slice. The times are simulated.
128 devices in a mesh: row: 16 (over z, y), col: 8 (over x, core).
Axes of the slice: x: 4, y: 4, z: 4, core: 2. Of those that a mesh axis runs over, the one named last changes fastest.
Arguments:
- forcing: float32 [2, 512, 16384], P(None, 'col', 'row'), may hold values from -170 to 170
- medium_index: int32 [512, 16384], P('col', 'row'), may hold values from 0 to 7
- absorbing_mask: int32 [512, 16384], P('col', 'row'), may hold values 0 or 1
- source_rows: int32 [16], replicated, may hold values from 0 to 511
- source_cols: int32 [16], replicated, may hold values from 0 to 16383
- refraction: float32 [8], replicated, may hold values from 0.6 to 1.8
- lift_weight: float32 [4, 64], replicated, may hold values from -3 to 3
- lift_bias: float32 [64], replicated, may hold values from -3 to 3
- spectral_weight: bfloat16 [2, 256, 64, 64], replicated, may hold values from -1.5 to 1.5
- point_weight: bfloat16 [64, 64], replicated, may hold values from -0.75 to 0.75
- layer_bias: float32 [64], replicated, may hold values from -3 to 3
- project_weight: bfloat16 [64, 2], replicated, may hold values from -0.75 to 0.75
Outputs:
- solution: float32 [2, 512, 16384], P(None, 'col', 'row')
- residual: float32 [2, 512, 16384], P(None, 'col', 'row')
All inputs are finite; a program needn't handle non-finite values. No bound on the sum of `absorbing_mask` on one device may be relied on, other than what follows from the above.
Results may differ from a plain program's by a relative error of at most 0.015.
Values sent between devices are 32-bit elements; how exact they have to be, the bound alone decides.
A program may use at most 192 MiB of HBM per device.

v0:
```python
import math

import jax
import jax.numpy as jnp
from jax import lax
from jax.sharding import PartitionSpec as P

K = 256


wave_base = 0.23
source_gain = 8.0
norm_eps = 1e-06


def padded_2(shard, sides, width):
    for axis, dim in sides:
        size, length = (lax.axis_size(axis), shard.shape[dim])
        up = [(i, (i + 1) % size) for i in range(size - 1)]
        down = [(j, i) for i, j in up]
        last = lax.slice_in_dim(shard, length - width, length, axis=dim)
        first = lax.slice_in_dim(shard, 0, width, axis=dim)
        before = lax.ppermute(last, axis, up)
        after = lax.ppermute(first, axis, down)
        shard = jnp.concatenate([before, shard, after], axis=dim)
    return shard


def forward_table(row_count, kept_modes, grid_length):
    positions = jnp.arange(row_count, dtype=jnp.int32)
    mode_index = jnp.arange(kept_modes, dtype=jnp.int32)
    phases = positions[:, None] * mode_index[None, :] % grid_length
    angles = phases.astype(jnp.float32) * jnp.float32(2.0 * math.pi / grid_length)
    factor = jnp.float32(1.0 / math.sqrt(grid_length))
    return jnp.concatenate([jnp.cos(angles) * factor, -jnp.sin(angles) * factor], axis=1)


def inverse_table(row_count, kept_modes, grid_length):
    positions = jnp.arange(row_count, dtype=jnp.int32)
    mode_index = jnp.arange(kept_modes, dtype=jnp.int32)
    phases = mode_index[:, None] * positions[None, :] % grid_length
    angles = phases.astype(jnp.float32) * jnp.float32(2.0 * math.pi / grid_length)
    factor = jnp.where(mode_index == 0, 1.0, 2.0).astype(jnp.float32) * jnp.float32(
        1.0 / math.sqrt(grid_length)
    )
    return jnp.concatenate(
        [jnp.cos(angles) * factor[:, None], -jnp.sin(angles) * factor[:, None]], axis=0
    ).astype(jnp.bfloat16)


def partial_modes(fields, table):
    line_count = fields.shape[1]
    result = jnp.dot(
        fields.reshape(2 * line_count, fields.shape[2]), table, precision=lax.Precision.HIGHEST
    )
    return result.reshape(2, line_count, table.shape[1])


def lift_modes(all_modes, lift_weight, lift_bias, grid_length):
    line_count = all_modes.shape[0]
    kept_modes = all_modes.shape[2] // 2
    channels = all_modes.reshape(line_count, 4, 2, kept_modes).transpose(0, 3, 2, 1)
    lifted = (
        channels[..., 0:1] * lift_weight[0]
        + channels[..., 1:2] * lift_weight[1]
        + channels[..., 2:3] * lift_weight[2]
        + channels[..., 3:4] * lift_weight[3]
    )
    mode_index = jnp.arange(kept_modes, dtype=jnp.int32)[:, None, None]
    plane_index = jnp.arange(2, dtype=jnp.int32)[None, :, None]
    at_anchor = ((mode_index == 0) & (plane_index == 0)).astype(lifted.dtype)
    lifted = lifted + at_anchor * (lift_bias * jnp.float32(math.sqrt(grid_length)))
    return lifted.reshape(line_count, kept_modes, 2 * lift_bias.shape[0]).astype(jnp.bfloat16)


def mode_weights(spectral_weight):
    real_part = spectral_weight[0]
    imag_part = spectral_weight[1]
    upper = jnp.concatenate([real_part, imag_part], axis=2)
    lower_half = jnp.concatenate([-imag_part, real_part], axis=2)
    return jnp.concatenate([upper, lower_half], axis=1)


def layer_block(fields, mode_mix, back_table, weights):
    lift_weight, lift_bias, point_weight, layer_bias, project_weight = weights
    line_count, kept_modes, double_width = mode_mix.shape
    channel_width = double_width // 2
    spectra = mode_mix.reshape(line_count, kept_modes, 2, channel_width).transpose(0, 3, 2, 1)
    spectra = spectra.reshape(line_count, channel_width, 2 * kept_modes)
    spectral = jnp.einsum("lcm,my->lcy", spectra, back_table, preferred_element_type=jnp.float32)
    lifted_field = (
        lift_weight[0][None, :, None] * fields[0][:, None, :]
        + lift_weight[1][None, :, None] * fields[1][:, None, :]
        + lift_weight[2][None, :, None] * fields[2][:, None, :]
        + lift_weight[3][None, :, None] * fields[3][:, None, :]
        + lift_bias[None, :, None]
    ).astype(jnp.bfloat16)
    pointwise = jnp.einsum(
        "cd,lcy->ldy", point_weight, lifted_field, preferred_element_type=jnp.float32
    )
    activation = jax.nn.gelu(
        pointwise + spectral + layer_bias[None, :, None], approximate=False
    ).astype(jnp.bfloat16)
    return jnp.einsum("cg,lcy->gly", project_weight, activation, preferred_element_type=jnp.float32)


def run_layer(fields, mode_mix, back_table, weights):
    line_count = fields.shape[1]
    grid_length = fields.shape[2]
    channel_width = mode_mix.shape[2] // 2
    block_size = math.gcd(line_count, max(1, 2**21 // (channel_width * grid_length)))
    block_count = line_count // block_size
    stacked_fields = fields.reshape(4, block_count, block_size, grid_length).transpose(1, 0, 2, 3)
    stacked_modes = mode_mix.reshape(block_count, block_size, mode_mix.shape[1], mode_mix.shape[2])

    def one_block(inputs):
        return layer_block(inputs[0], inputs[1], back_table, weights)

    result = lax.map(one_block, (stacked_fields, stacked_modes))
    return result.transpose(1, 0, 2, 3).reshape(2, line_count, grid_length)


def apply_operator(padded, grid_field, wave_factor, damping):
    edge_sum = (
        padded[:, 2:, 1:-1] + padded[:, :-2, 1:-1] + padded[:, 1:-1, 2:] + padded[:, 1:-1, :-2]
    )
    corner = padded[:, 2:, 2:] + padded[:, 2:, :-2] + padded[:, :-2, 2:] + padded[:, :-2, :-2]
    laplace = (4.0 * edge_sum + corner - 20.0 * grid_field) / 6.0
    real_plane = -laplace[0] - wave_factor * (grid_field[0] + damping * grid_field[1])
    imag_plane = -laplace[1] - wave_factor * (grid_field[1] - damping * grid_field[0])
    return jnp.stack([real_plane, imag_plane])


def inner_pair(first_field, second_field):
    real_sum = jnp.sum(first_field[0] * second_field[0] + first_field[1] * second_field[1])
    imag_sum = jnp.sum(first_field[0] * second_field[1] - first_field[1] * second_field[0])
    return (real_sum, imag_sum)


def complex_scale(real_part, imag_part, grid_field):
    return jnp.stack(
        [
            real_part * grid_field[0] - imag_part * grid_field[1],
            real_part * grid_field[1] + imag_part * grid_field[0],
        ]
    )


def squared_total(grid_field):
    return lax.psum(jnp.sum(grid_field * grid_field), ("row", "col"))


def small_solve(initial_norm, top_left, lower_left, top_right, middle_right, lower_right):
    a_re, a_im = top_left
    b_re, b_im = top_right
    d_re, d_im = middle_right
    gram_first = a_re * a_re + a_im * a_im + lower_left * lower_left
    gram_second = b_re * b_re + b_im * b_im + d_re * d_re + d_im * d_im + lower_right * lower_right
    cross_re = a_re * b_re + a_im * b_im + lower_left * d_re
    cross_im = a_re * b_im - a_im * b_re + lower_left * d_im
    minor_re = a_re * d_re - a_im * d_im - b_re * lower_left
    minor_im = a_re * d_im + a_im * d_re - b_im * lower_left
    determinant = (
        minor_re * minor_re
        + minor_im * minor_im
        + (a_re * a_re + a_im * a_im) * lower_right * lower_right
        + lower_left * lower_left * lower_right * lower_right
    )
    first_re = initial_norm * a_re
    first_im = -initial_norm * a_im
    second_re = initial_norm * b_re
    second_im = -initial_norm * b_im
    coef0_re = (
        gram_second * first_re - (cross_re * second_re - cross_im * second_im)
    ) / determinant
    coef0_im = (
        gram_second * first_im - (cross_re * second_im + cross_im * second_re)
    ) / determinant
    coef1_re = (gram_first * second_re - (cross_re * first_re + cross_im * first_im)) / determinant
    coef1_im = (gram_first * second_im - (cross_re * first_im - cross_im * first_re)) / determinant
    rest0_re = initial_norm - (
        a_re * coef0_re - a_im * coef0_im + b_re * coef1_re - b_im * coef1_im
    )
    rest0_im = -(a_re * coef0_im + a_im * coef0_re + b_re * coef1_im + b_im * coef1_re)
    rest1_re = -(lower_left * coef0_re + d_re * coef1_re - d_im * coef1_im)
    rest1_im = -(lower_left * coef0_im + d_re * coef1_im + d_im * coef1_re)
    rest2_re = -lower_right * coef1_re
    rest2_im = -lower_right * coef1_im
    return (
        (coef0_re, coef0_im),
        (coef1_re, coef1_im),
        (rest0_re, rest0_im),
        (rest1_re, rest1_im),
        (rest2_re, rest2_im),
    )


def shards(
    forcing,
    medium_index,
    absorbing_mask,
    source_rows,
    source_cols,
    refraction,
    lift_weight,
    lift_bias,
    spectral_weight,
    point_weight,
    layer_bias,
    project_weight,
):
    tile_rows = forcing.shape[1]
    tile_cols = forcing.shape[2]
    grid_rows = tile_rows * lax.axis_size("col")
    grid_cols = tile_cols * lax.axis_size("row")
    first_line = lax.axis_index("col") * tile_rows
    first_col = lax.axis_index("row") * tile_cols
    line_hits = (
        source_rows[:, None] == first_line + jnp.arange(tile_rows, dtype=jnp.int32)[None, :]
    ).astype(jnp.float32)
    col_hits = (
        source_cols[:, None] == first_col + jnp.arange(tile_cols, dtype=jnp.int32)[None, :]
    ).astype(jnp.float32)
    source_count = jnp.dot(
        line_hits.T, col_hits, precision=lax.Precision.HIGHEST, preferred_element_type=jnp.float32
    )
    right_side = jnp.stack([forcing[0] + source_gain * source_count, forcing[1]])
    refractive = jnp.zeros((tile_rows, tile_cols), jnp.float32)
    for level_index in range(refraction.shape[0]):
        refractive = refractive + jnp.where(
            medium_index == level_index, refraction[level_index], 0.0
        )
    damping = 0.1 + absorbing_mask.astype(jnp.float32)
    wave_factor = wave_base * refractive * (wave_base * refractive)
    features = jnp.stack([refractive, damping])
    big_weights = mode_weights(spectral_weight)
    grid_scale = jnp.float32(math.sqrt(grid_rows * grid_cols))
    weights = (lift_weight, lift_bias, point_weight, layer_bias, project_weight)
    forward = forward_table(grid_cols, K, grid_cols)
    back_table = inverse_table(grid_cols, K, grid_cols)
    feature_lines = lax.all_to_all(features, "row", split_axis=1, concat_axis=2, tiled=True)
    feature_modes = partial_modes(feature_lines, forward).transpose(1, 0, 2)
    initial_norm = jnp.sqrt(squared_total(right_side) + norm_eps)
    krylov_basis = [right_side / initial_norm]
    corrections = []
    products_all = []
    subdiagonals = []
    for column in range(2):
        scaled = krylov_basis[column] * grid_scale
        scaled_lines = lax.all_to_all(scaled, "row", split_axis=1, concat_axis=2, tiled=True)
        wave_modes = partial_modes(scaled_lines, forward).transpose(1, 0, 2)
        lifted = lift_modes(
            jnp.concatenate([wave_modes, feature_modes], axis=1), lift_weight, lift_bias, grid_cols
        )
        mode_mix = jnp.einsum(
            "lkc,kcd->lkd", lifted, big_weights, preferred_element_type=jnp.float32
        ).astype(jnp.bfloat16)
        line_result = run_layer(
            jnp.concatenate([scaled_lines, feature_lines], axis=0), mode_mix, back_table, weights
        )
        correction = lax.all_to_all(line_result, "row", split_axis=2, concat_axis=1, tiled=True)
        corrections.append(correction)
        padded = padded_2(correction, (("row", 2), ("col", 1)), 1)
        applied = apply_operator(padded, correction, wave_factor, damping)
        products = []
        for earlier in range(column + 1):
            real_sum, imag_sum = inner_pair(krylov_basis[earlier], applied)
            summed_re, summed_im = lax.psum((real_sum, imag_sum), ("row", "col"))
            applied = applied - complex_scale(summed_re, summed_im, krylov_basis[earlier])
            products.append((summed_re, summed_im))
        subdiagonal = jnp.sqrt(squared_total(applied) + norm_eps)
        krylov_basis.append(applied / subdiagonal)
        products_all.append(products)
        subdiagonals.append(subdiagonal)
    coef0, coef1, rest0, rest1, rest2 = small_solve(
        initial_norm,
        products_all[0][0],
        subdiagonals[0],
        products_all[1][0],
        products_all[1][1],
        subdiagonals[1],
    )
    solution = complex_scale(coef0[0], coef0[1], corrections[0]) + complex_scale(
        coef1[0], coef1[1], corrections[1]
    )
    residual = (
        complex_scale(rest0[0], rest0[1], krylov_basis[0])
        + complex_scale(rest1[0], rest1[1], krylov_basis[1])
        + complex_scale(rest2[0], rest2[1], krylov_basis[2])
    )
    return (solution, residual)


def solution(mesh):
    return jax.shard_map(
        shards,
        mesh=mesh,
        in_specs=(
            P(None, "col", "row"),
            P("col", "row"),
            P("col", "row"),
            P(),
            P(),
            P(),
            P(),
            P(),
            P(),
            P(),
            P(),
            P(),
        ),
        out_specs=(P(None, "col", "row"), P(None, "col", "row")),
        check_vma=False,
    )
```

profile of v0, /device:TPU:1, one launch (start us, length us, event | category | flops | bytes accessed | tf_op | source)
XLA Modules:
  0.0 1129.2 jit_solution(11224591183513585736)
XLA Ops:
  3.7 68.7 %psum.63 = f32[]{:T(128)} all-reduce(f32[]{:T(128)} %multiply_reduce_fusion.2), channel_id=1, replica_groups=mesh['row'=16,'col'=8] {'row','col'}, use_global_device_ids=true, to_apply=%region_1.2 | all-reduce | flops 1 | bytes 8 | tf_op jit(solution)/shard_map/psum | solution.py:150
  75.2 3.9 all-to-all-start
  79.1 68.3 %negate_multiply_fusion.2 = (f32[16384,256]{1,0:T(8,128)}, f32[16384,256]{1,0:T(8,128)}) fusion(), kind=kLoop, calls=%fused_computation.185 | loop fusion | flops 71303168 | bytes 33554432 | tf_op jit(solution)/shard_map/mul | solution.py:35
  148.1 68.3 %multiply_convert_fusion.1 = (bf16[256,16384]{1,0:T(8,128)(2,1)S(1)}, bf16[256,16384]{1,0:T(8,128)(2,1)S(1)}) fusion(f32[256]{0:T(256)S(1)} %select_multiply_fusion), kind=kLoop, calls=%fused_computation.182 | loop fusion | flops 79691776 | bytes 16778240 | tf_op jit(solution)/shard_map/convert
  216.5 7.5 pad_maximum_fusion
  224.0 5.4 fusion.196
  230.7 1.7 fusion.212
  232.4 6.9 all-to-all-start.1
  239.8 7.5 copy.152
  247.3 6.7 copy.151
  254.1 4.8 bitcast_negate_fusion
  261.9 20.5 %fusion.136 = f32[4,2,512]{2,0,1:T(4,128)S(1)} fusion(f32[2,4,16384]{2,1,0:T(4,128)S(1)} %dot_general.49, f32[16384,256]{1,0:T(8,128)} %get-tuple-element.348, f32[16384,256]{1,0:T(8,128)} %get-tuple-element.349), kind=kOutput, calls=%fused_computation.198 | convolution fusion | flops 813694976 | bytes 34095104 | tf_op jit(solution)/shard_map/dot_general | solution.py:53
  282.4 20.9 %fusion.135 = f32[4,2,512]{2,0,1:T(4,128)S(1)} fusion(f32[2,4,16384]{2,1,0:T(4,128)S(1)} %dot_general.47, f32[16384,256]{1,0:T(8,128)} %get-tuple-element.348, f32[16384,256]{1,0:T(8,128)} %get-tuple-element.349), kind=kOutput, calls=%fused_computation.197 | convolution fusion | flops 813694976 | bytes 34095104 | tf_op jit(solution)/shard_map/dot_general | solution.py:53
  304.4 8.8 convolution_convert_fusion.1
  313.4 68.2 %while.20 = (s32[]{:T(128)}, f32[2,2,2,16384]{3,1,2,0:T(2,128)S(1)}, f32[4,64]{1,0:T(4,128)S(1)}, f32[2,4,2,16384]{3,2,0,1:T(2,128)S(1)}, f32[64]{0:T(128)S(1)},...) while((s32[]{:T(128)}, ...), condition=%wide.region_3.4_spmd, body=%wide.region_2.3_spmd.sunk | while | flops 2603614208 | bytes 56242304 | solution.py:119
  313.9 8.1 fusion.245
  322.0 5.1 fusion.246
  327.2 20.4 %fusion.247 = f32[2,2,2,16384]{3,1,2,0:T(2,128)S(1)} fusion(f32[2,2,2,16384]{3,1,2,0:T(2,128)S(1)} %get-tuple-element.524, s32[]{:T(128)S(6)} %copy.173, f32[2,64,16384]{2,1,0:T(8,128)S(1)} %get-tuple-element.490, u8[64,16384]{1,0:T(8,128)(4,1)S(1)} %get-tuple-element.491, bf16[64,2]{0,1:T(2,128)(2,1)S(1)} %get-tuple-element.543), kind=kOutput, calls=%fused_computation.4.clone.1 | convolution fusion | flops 150994944 | bytes 9699844 | tf_op jit(solution)/shard_map/while/body/eval_jaxpr/cg,lcy->gly/dot_general | solution.py:104
  347.9 8.1 fusion.245
  356.0 5.1 fusion.246
  361.2 20.4 %fusion.247 = f32[2,2,2,16384]{3,1,2,0:T(2,128)S(1)} fusion(f32[2,2,2,16384]{3,1,2,0:T(2,128)S(1)} %get-tuple-element.524, s32[]{:T(128)S(6)} %copy.173, f32[2,64,16384]{2,1,0:T(8,128)S(1)} %get-tuple-element.490, u8[64,16384]{1,0:T(8,128)(4,1)S(1)} %get-tuple-element.491, bf16[64,2]{0,1:T(2,128)(2,1)S(1)} %get-tuple-element.543), kind=kOutput, calls=%fused_computation.4.clone.1 | convolution fusion | flops 150994944 | bytes 9699844 | tf_op jit(solution)/shard_map/while/body/eval_jaxpr/cg,lcy->gly/dot_general | solution.py:104
  381.6 14.8 %copy.124 = f32[2,4,16384]{1,0,2:T(2,128)} copy(f32[2,4,16384]{2,0,1:T(2,128)S(1)} %bitcast.400) | data formatting | bytes 1048576 | tf_op jit(solution)/shard_map/reshape | solution.py:120
  396.4 27.0 %reshape.332 = f32[16,1,8192]{2,1,0:T(1,128)S(1)} reshape(f32[16384,2,4]{2,1,0:T(2,128)} %bitcast.365) | data formatting | bytes 1048576
  423.4 16.2 %all_to_all.81 = f32[16,1,8192]{2,1,0:T(1,128)S(1)} all-to-all(f32[16,1,8192]{2,1,0:T(1,128)S(1)} %reshape.332), channel_id=1, replica_groups=mesh['row'=16,'col'=8] {'row'}, dimensions={0} | all-to-all | bytes 1048576 | tf_op jit(solution)/shard_map/all_to_all | solution.py:261
  440.1 1.8 reduce.6
  441.9 32.0 %reshape.333 = f32[16384,2,4]{2,1,0:T(2,128)} reshape(f32[16,8192]{1,0:T(8,128)S(1)} %reduce.6) | data formatting | bytes 1048576
  473.9 13.4 %copy.145 = f32[2,4,16,1024]{3,2,1,0:T(8,128)S(1)} copy(f32[2,4,16,1024]{1,0,3,2:T(2,128)} %bitcast.366) | data formatting | bytes 1048576 | tf_op jit(solution)/shard_map/all_to_all | solution.py:261
  489.3 4.0 collective-permute-start
  495.6 6.1 collective-permute-start.2
  501.7 1.9 collective-permute-start.3
  505.9 1.9 fusion.159
  507.8 6.2 fusion.189
  514.0 66.9 %all-reduce.2 = (f32[]{:T(128)}, f32[]{:T(128)}) all-reduce(f32[]{:T(128)} %get-tuple-element.219, f32[]{:T(128)} %get-tuple-element.218), channel_id=1, replica_groups=mesh['row'=16,'col'=8] {'row','col'}, use_global_device_ids=true, to_apply=%region_7.8 | all-reduce | flops 2 | bytes 16 | tf_op jit(solution)/shard_map/psum | solution.py:268
  580.9 1.3 multiply_subtract_fusion.7
  583.0 62.6 %psum.66 = f32[]{:T(128)} all-reduce(f32[]{:T(128)} %multiply_reduce_fusion.1), channel_id=1, replica_groups=mesh['row'=16,'col'=8] {'row','col'}, use_global_device_ids=true, to_apply=%region_9.10 | all-reduce | flops 1 | bytes 8 | tf_op jit(solution)/shard_map/psum | solution.py:150
  647.6 14.6 %all_to_all.82 = f32[2,64,1024]{2,0,1:T(2,128)S(1)} all-to-all(f32[2,64,1024]{2,0,1:T(2,128)S(1)} %copy.129), channel_id=1, replica_groups=mesh['row'=16,'col'=8] {'row'}, dimensions={1} | all-to-all | bytes 1048576 | tf_op jit(solution)/shard_map/all_to_all | solution.py:250
  663.3 20.5 %fusion.137 = f32[4,2,512]{2,0,1:T(4,128)S(1)} fusion(f32[2,4,16384]{2,1,0:T(4,128)S(1)} %dot_general.52, f32[16384,256]{1,0:T(8,128)} %get-tuple-element.348, f32[16384,256]{1,0:T(8,128)} %get-tuple-element.349), kind=kOutput, calls=%fused_computation.199 | convolution fusion | flops 813694976 | bytes 34095104 | tf_op jit(solution)/shard_map/dot_general | solution.py:53
  685.0 8.8 convolution_convert_fusion
  694.0 68.2 %while.21 = (s32[]{:T(128)}, f32[2,2,2,16384]{3,1,2,0:T(2,128)S(1)}, f32[4,64]{1,0:T(4,128)S(1)}, f32[2,4,2,16384]{3,2,0,1:T(2,128)S(1)}, f32[64]{0:T(128)S(1)},...) while((s32[]{:T(128)}, ...), condition=%wide.region_11.12_spmd, body=%wide.region_10.11_spmd.sunk | while | flops 2603614208 | bytes 56242304 | solution.py:119
  694.5 8.1 fusion.252
  702.6 5.1 fusion.253
  707.8 20.4 %fusion.254 = f32[2,2,2,16384]{3,1,2,0:T(2,128)S(1)} fusion(f32[2,2,2,16384]{3,1,2,0:T(2,128)S(1)} %get-tuple-element.557, s32[]{:T(128)S(6)} %copy.179, f32[2,64,16384]{2,1,0:T(8,128)S(1)} %get-tuple-element.510, u8[64,16384]{1,0:T(8,128)(4,1)S(1)} %get-tuple-element.511, bf16[64,2]{0,1:T(2,128)(2,1)S(1)} %get-tuple-element.576), kind=kOutput, calls=%fused_computation.86.clone.1 | convolution fusion | flops 150994944 | bytes 9699844 | tf_op jit(solution)/shard_map/while/body/eval_jaxpr/cg,lcy->gly/dot_general | solution.py:104
  728.5 8.1 fusion.252
  736.7 5.1 fusion.253
  741.8 20.4 %fusion.254 = f32[2,2,2,16384]{3,1,2,0:T(2,128)S(1)} fusion(f32[2,2,2,16384]{3,1,2,0:T(2,128)S(1)} %get-tuple-element.557, s32[]{:T(128)S(6)} %copy.179, f32[2,64,16384]{2,1,0:T(8,128)S(1)} %get-tuple-element.510, u8[64,16384]{1,0:T(8,128)(4,1)S(1)} %get-tuple-element.511, bf16[64,2]{0,1:T(2,128)(2,1)S(1)} %get-tuple-element.576), kind=kOutput, calls=%fused_computation.86.clone.1 | convolution fusion | flops 150994944 | bytes 9699844 | tf_op jit(solution)/shard_map/while/body/eval_jaxpr/cg,lcy->gly/dot_general | solution.py:104
  762.2 14.8 %copy.135 = f32[2,4,16384]{1,0,2:T(2,128)} copy(f32[2,4,16384]{2,0,1:T(2,128)S(1)} %bitcast.399) | data formatting | bytes 1048576 | tf_op jit(solution)/shard_map/reshape | solution.py:120
  777.1 27.0 %reshape.334 = f32[16,1,8192]{2,1,0:T(1,128)S(1)} reshape(f32[16384,2,4]{2,1,0:T(2,128)} %bitcast.367) | data formatting | bytes 1048576
  804.1 13.1 %all_to_all.83 = f32[16,1,8192]{2,1,0:T(1,128)S(1)} all-to-all(f32[16,1,8192]{2,1,0:T(1,128)S(1)} %reshape.334), channel_id=1, replica_groups=mesh['row'=16,'col'=8] {'row'}, dimensions={0} | all-to-all | bytes 1048576 | tf_op jit(solution)/shard_map/all_to_all | solution.py:261
  817.1 1.8 reduce.7
  819.0 32.1 %reshape.335 = f32[16384,2,4]{2,1,0:T(2,128)} reshape(f32[16,8192]{1,0:T(8,128)S(1)} %reduce.7) | data formatting | bytes 1048576
  851.0 13.4 %copy.146 = f32[2,4,16,1024]{3,2,1,0:T(8,128)S(1)} copy(f32[2,4,16,1024]{1,0,3,2:T(2,128)} %bitcast.368) | data formatting | bytes 1048576 | tf_op jit(solution)/shard_map/all_to_all | solution.py:261
  866.4 4.0 collective-permute-start.4
  875.8 5.1 collective-permute-start.6
  880.9 1.9 collective-permute-start.7
  884.5 1.7 squeeze.71
  886.2 1.8 copy.139
  888.0 1.7 squeeze.72
  889.8 1.9 fusion.145
  891.6 7.3 fusion.195
  899.0 64.7 %all-reduce.1 = (f32[]{:T(128)}, f32[]{:T(128)}) all-reduce(f32[]{:T(128)} %get-tuple-element.217, f32[]{:T(128)} %get-tuple-element.216), channel_id=1, replica_groups=mesh['row'=16,'col'=8] {'row','col'}, use_global_device_ids=true, to_apply=%region_13.14 | all-reduce | flops 2 | bytes 16 | tf_op jit(solution)/shard_map/psum | solution.py:268
  973.7 1.3 multiply_subtract_fusion.6
  975.8 62.7 %all-reduce = (f32[]{:T(128)}, f32[]{:T(128)}) all-reduce(f32[]{:T(128)} %get-tuple-element.215, f32[]{:T(128)} %get-tuple-element.214), channel_id=1, replica_groups=mesh['row'=16,'col'=8] {'row','col'}, use_global_device_ids=true, to_apply=%region_17.18 | all-reduce | flops 2 | bytes 16 | tf_op jit(solution)/shard_map/psum | solution.py:268
  1050.1 64.2 %psum.71 = f32[]{:T(128)} all-reduce(f32[]{:T(128)} %multiply_reduce_fusion), channel_id=1, replica_groups=mesh['row'=16,'col'=8] {'row','col'}, use_global_device_ids=true, to_apply=%region_21.22 | all-reduce | flops 1 | bytes 8 | tf_op jit(solution)/shard_map/psum | solution.py:150
  1122.6 1.8 broadcast_divide_fusion
  (206 shorter events, 37.2 us)
Async XLA Ops:
  75.2 157.2 %all-to-all-start = ((f32[2,64,1024]{2,0,1:T(2,128)}), f32[2,64,1024]{2,0,1:T(2,128)S(1)}, u32[]{:S(2)}, u32[]{:S(2)}) async-start(f32[2,64,1024]{2,0,1:T(2,128)} %copy.114), calls=%async_computation | async-start | bytes 1048576 | tf_op jit(solution)/shard_map/all_to_all | solution.py:250
  79.1 68.3 %copy-start.20 = (f32[4,64]{1,0:T(4,128)S(1)}, f32[4,64]{1,0:T(4,128)}, u32[]{:S(2)}) copy-start(f32[4,64]{1,0:T(4,128)} %param.22) | copy-start | bytes 3076
  79.1 68.3 %copy-start.23 = (f32[8]{0:T(128)S(1)}, f32[8]{0:T(128)}, u32[]{:S(2)}) copy-start(f32[8]{0:T(128)} %param.21) | copy-start | bytes 100
  216.5 7.5 copy-start.8
  216.5 7.5 copy-start.11
  216.5 14.2 %copy-start.7 = (bf16[2,256,64,64]{1,3,2,0:T(8,128)(2,1)S(1)}, bf16[2,256,64,64]{1,3,2,0:T(8,128)(2,1)}, u32[]{:S(2)}) copy-start(bf16[2,256,64,64]{1,3,2,0:T(8,128)(2,1)} %param.24) | copy-start | bytes 12582916
  224.0 15.3 %copy-start.35 = (f32[64]{0:T(128)S(1)}, f32[64]{0:T(128)}, u32[]{:S(2)}) copy-start(f32[64]{0:T(128)} %param.23) | copy-start | bytes 772
  224.0 15.8 %copy-start.24 = (bf16[64,64]{1,0:T(8,128)(2,1)S(1)}, bf16[64,64]{1,0:T(8,128)(2,1)}, u32[]{:S(2)}) copy-start(bf16[64,64]{1,0:T(8,128)(2,1)} %param.25) | copy-start | bytes 24580
  232.4 28.4 %all-to-all-start.1 = ((f32[2,64,1024]{2,0,1:T(2,128)}), f32[2,64,1024]{2,0,1:T(2,128)S(1)}, u32[]{:S(2)}, u32[]{:S(2)}) async-start(f32[2,64,1024]{2,0,1:T(2,128)} %copy.116), calls=%async_computation.1 | async-start | bytes 1048576 | tf_op jit(solution)/shard_map/all_to_all | solution.py:241
  239.5 63.9 %copy-start.27 = (f32[128]{0:T(128)}, f32[128]{0:T(128)S(1)}, u32[]{:S(2)}) copy-start(f32[128]{0:T(128)S(1)} %mul.989) | copy-start | bytes 1540
  239.5 63.8 %copy-start.29 = (f32[128]{0:T(128)}, f32[128]{0:T(128)S(1)}, u32[]{:S(2)}) copy-start(f32[128]{0:T(128)S(1)} %mul.1013) | copy-start | bytes 1540
  239.6 63.8 %copy-start.31 = (f32[128]{0:T(128)}, f32[128]{0:T(128)S(1)}, u32[]{:S(2)}) copy-start(f32[128]{0:T(128)S(1)} %mul.1005) | copy-start | bytes 1540
  239.7 63.7 %copy-start.33 = (f32[128]{0:T(128)}, f32[128]{0:T(128)S(1)}, u32[]{:S(2)}) copy-start(f32[128]{0:T(128)S(1)} %mul.997) | copy-start | bytes 1540
  254.1 49.4 %copy-start.16 = (f32[256,128]{0,1:T(8,128)}, f32[256,128]{0,1:T(8,128)S(1)}, u32[]{:S(2)}) copy-start(f32[256,128]{0,1:T(8,128)S(1)} %bitcast_multiply_fusion.16) | copy-start | bytes 393220
  261.5 42.3 %copy-start.5 = (f32[2,2,2,16384]{3,2,1,0:T(2,128)}, f32[2,2,2,16384]{3,2,1,0:T(2,128)S(1)}, u32[]{:S(2)}) copy-start(f32[2,2,2,16384]{3,2,1,0:T(2,128)S(1)} %concatenate.77) | copy-start | bytes 1572868
  282.4 20.9 %copy-start.21 = (f32[4,2,512]{2,0,1:T(4,128)}, f32[4,2,512]{2,0,1:T(4,128)S(1)}, u32[]{:S(2)}) copy-start(f32[4,2,512]{2,0,1:T(4,128)S(1)} %fusion.136) | copy-start | bytes 49156
  282.4 21.5 %copy-start.15 = (f32[2,2,2,16384]{3,2,1,0:T(2,128)S(1)}, f32[2,2,2,16384]{3,2,1,0:T(2,128)}, u32[]{:S(2)}) copy-start(f32[2,2,2,16384]{3,2,1,0:T(2,128)} %concatenate.76) | copy-start | bytes 1572868
  304.4 8.9 copy-start.37
  304.4 8.9 copy-start.39
  381.6 14.8 %copy-start.25 = (bf16[64,64]{0,1:T(8,128)(2,1)}, bf16[64,64]{0,1:T(8,128)(2,1)S(1)}, u32[]{:S(2)}) copy-start(bf16[64,64]{0,1:T(8,128)(2,1)S(1)} %get-tuple-element.590) | copy-start | bytes 24580
  487.3 174.8 %copy-start.3 = (f32[2,4,16,1024]{3,2,1,0:T(8,128)}, f32[2,4,16,1024]{3,2,1,0:T(8,128)S(1)}, u32[]{:S(2)}) copy-start(f32[2,4,16,1024]{3,2,1,0:T(8,128)S(1)} %copy.145) | copy-start | bytes 1572868
  487.3 20.4 %copy-start = (f32[2,64,1024]{2,1,0:T(8,128)S(1)}, f32[2,64,1024]{2,1,0:T(8,128)}, u32[]{:S(2)}) copy-start(f32[2,64,1024]{2,1,0:T(8,128)} %get-tuple-element.273) | copy-start | bytes 1572868
  487.4 20.4 %copy-start.9 = (s32[64,1024]{1,0:T(8,128)S(1)}, s32[64,1024]{1,0:T(8,128)}, u32[]{:S(2)}) copy-start(s32[64,1024]{1,0:T(8,128)} %param.18) | copy-start | bytes 786436
  487.4 20.4 %copy-start.12 = (s32[64,1024]{1,0:T(8,128)S(1)}, s32[64,1024]{1,0:T(8,128)}, u32[]{:S(2)}) copy-start(s32[64,1024]{1,0:T(8,128)} %param.17) | copy-start | bytes 786436
  488.0 5.3 collective-permute-start.1
  489.3 5.3 collective-permute-start
  494.6 7.0 copy-start.19
  495.6 10.3 collective-permute-start.2
  501.7 4.2 collective-permute-start.3
  663.3 20.6 %copy-start.22 = (f32[4,2,512]{2,0,1:T(4,128)S(1)}, f32[4,2,512]{2,0,1:T(4,128)}, u32[]{:S(2)}) copy-start(f32[4,2,512]{2,0,1:T(4,128)} %copy-done.21) | copy-start | bytes 49156
  663.3 20.6 %copy-start.6 = (f32[2,2,2,16384]{3,2,1,0:T(2,128)S(1)}, f32[2,2,2,16384]{3,2,1,0:T(2,128)}, u32[]{:S(2)}) copy-start(f32[2,2,2,16384]{3,2,1,0:T(2,128)} %copy-done.5) | copy-start | bytes 1572868
  663.3 21.2 %copy-start.17 = (f32[256,128]{0,1:T(8,128)S(1)}, f32[256,128]{0,1:T(8,128)}, u32[]{:S(2)}) copy-start(f32[256,128]{0,1:T(8,128)} %copy-done.16) | copy-start | bytes 393220
  663.3 21.2 %copy-start.28 = (f32[128]{0:T(128)S(1)}, f32[128]{0:T(128)}, u32[]{:S(2)}) copy-start(f32[128]{0:T(128)} %copy-done.27) | copy-start | bytes 1540
  663.3 21.2 %copy-start.30 = (f32[128]{0:T(128)S(1)}, f32[128]{0:T(128)}, u32[]{:S(2)}) copy-start(f32[128]{0:T(128)} %copy-done.29) | copy-start | bytes 1540
  663.3 21.2 %copy-start.32 = (f32[128]{0:T(128)S(1)}, f32[128]{0:T(128)}, u32[]{:S(2)}) copy-start(f32[128]{0:T(128)} %copy-done.31) | copy-start | bytes 1540
  663.3 21.2 %copy-start.34 = (f32[128]{0:T(128)S(1)}, f32[128]{0:T(128)}, u32[]{:S(2)}) copy-start(f32[128]{0:T(128)} %copy-done.33) | copy-start | bytes 1540
  685.0 9.0 copy-start.26
  685.0 9.0 copy-start.36
  685.0 9.0 copy-start.38
  685.0 9.0 copy-start.40
  864.4 27.2 %copy-start.1 = (f32[2,64,1024]{2,1,0:T(8,128)S(1)}, f32[2,64,1024]{2,1,0:T(8,128)}, u32[]{:S(2)}) copy-start(f32[2,64,1024]{2,1,0:T(8,128)} %get-tuple-element.273) | copy-start | bytes 1572868
  864.4 27.2 %copy-start.10 = (s32[64,1024]{1,0:T(8,128)S(1)}, s32[64,1024]{1,0:T(8,128)}, u32[]{:S(2)}) copy-start(s32[64,1024]{1,0:T(8,128)} %param.18) | copy-start | bytes 786436
  864.4 110.6 %copy-start.2 = (f32[2,64,1024]{2,1,0:T(8,128)S(1)}, f32[2,64,1024]{2,1,0:T(8,128)}, u32[]{:S(2)}) copy-start(f32[2,64,1024]{2,1,0:T(8,128)} %get-tuple-element.269) | copy-start | bytes 1572868
  865.1 9.1 collective-permute-start.5
  866.4 7.8 collective-permute-start.4
  874.2 0.6 copy-start.18
  875.1 249.3 %copy-start.4 = (f32[2,4,16,1024]{3,2,1,0:T(8,128)S(1)}, f32[2,4,16,1024]{3,2,1,0:T(8,128)}, u32[]{:S(2)}) copy-start(f32[2,4,16,1024]{3,2,1,0:T(8,128)} %copy-done.3) | copy-start | bytes 1572868
  875.8 14.0 %collective-permute-start.6 = (f32[2,1,1026]{2,1,0:T(1,128)}, f32[2,1,1026]{2,1,0:T(1,128)S(1)}, u32[]{:S(2)}, u32[]{:S(2)}) collective-permute-start(f32[2,1,1026]{2,1,0:T(1,128)} %get-tuple-element.296), channel_id=1, source_target_pairs={{1,0},{2,1},{3,2},{4,3},{5,4},{6,5},{7,6},{9,8},{10,9},{11,10},{12... | collective-permute-start | bytes 24632 | tf_op jit(solution)/shard_map/ppermute | solution.py:24
  880.9 8.8 collective-permute-start.7
  1047.3 0.7 copy-start.13
  1124.5 3.3 copy-start.14
where the time goes:
time: 1140 us; the launch traced here: 1130 us
  blocking collectives  434 us (38%)
  local copies, waits for them, and re-layouts  218 us (19%)
  matrix products  215 us (19%)
  other arithmetic  190 us (17%)
  starting transfers between devices  36.4 us (3%)
  between operations  34.6 us (3%)
    psum x3, blocking collectives, squared_total(): return lax.psum(jnp.sum(grid_field * grid_field), ('row', 'col'))  195 us
    psum x3, blocking collectives, shards(): summed_re, summed_im = lax.psum((real_sum, imag_sum), ('row', 'col'))  194 us
    unnamed x89, local copies, waits for them, and re-layouts  135 us
    dot_general x4, matrix products, layer_block(): jnp.einsum('cg,lcy->gly', project_weight, activation, preferred_element_t...  81.7 us
    mul x1, other arithmetic, forward_table(): -jnp.sin(angles) * factor  68.3 us
    another operation x1, other arithmetic  68.3 us
    dot_general x3, matrix products, partial_modes(): jnp.dot(fields.reshape(2 * line_count, fields.shape[2]), table, precision...  61.9 us
    dot_general x4, matrix products, layer_block(): jnp.einsum('lcm,my->lcy', spectra, back_table, preferred_element_type=jnp...  32.5 us
  transfers between devices with their start and end apart: 10, of which 1 were waited for; matrix products, arithmetic and copies ran while one was open for 16% of the time, Pallas kernels for 0%

commit v1 on v0

v1 whole, which is shorter than its diff:
```python
import functools
import math

import jax
import jax.numpy as jnp
import numpy as np
import ml_dtypes
from jax import lax
from jax.experimental import pallas as pl
from jax.experimental.pallas import tpu as pltpu
from jax.sharding import PartitionSpec as P

K = 256

wave_base = 0.23
source_gain = 8.0
norm_eps = 1e-06

MESH = pl.DeviceIdType.MESH
F32 = jnp.float32
BF16 = jnp.bfloat16
LINES = 16
SLABS = 16
PIECE = 256


def base_tables(tile_cols, kept_modes, grid_cols):
    positions = np.arange(tile_cols, dtype=np.int64)
    mode_index = np.arange(kept_modes, dtype=np.int64)
    angles = (positions[:, None] * mode_index[None, :] % grid_cols) * (2.0 * math.pi / grid_cols)
    scale = 1.0 / math.sqrt(grid_cols)
    table = np.concatenate([np.cos(angles), -np.sin(angles)], axis=1) * scale
    high = table.astype(np.float32).astype(ml_dtypes.bfloat16)
    low = (table - high.astype(np.float64)).astype(np.float32).astype(ml_dtypes.bfloat16)
    return high, low, np.ascontiguousarray(high.T)


def phase_table(row_count, kept_modes):
    tile = np.arange(row_count, dtype=np.int64)
    mode_index = np.arange(kept_modes, dtype=np.int64)
    angles = (tile[:, None] * mode_index[None, :] % row_count) * (2.0 * math.pi / row_count)
    table = np.concatenate([np.cos(angles), np.sin(angles)], axis=1).astype(np.float32)
    return np.ascontiguousarray(np.broadcast_to(table[:, None, :], (row_count, 8, 2 * kept_modes)))


def split(x):
    high = x.astype(BF16)
    return high, (x - high.astype(F32)).astype(BF16)


def gelu(x):
    return 0.5 * x * (1.0 + lax.erf(x * math.sqrt(0.5)))


def cmul(a, b):
    return a[0] * b[0] - a[1] * b[1], a[0] * b[1] + a[1] * b[0]


def conj_cmul(a, b):
    return a[0] * b[0] + a[1] * b[1], a[0] * b[1] - a[1] * b[0]


def small_solve(beta, a, b, c, d, e):
    gram_first = a[0] * a[0] + a[1] * a[1] + c * c
    gram_second = b[0] * b[0] + b[1] * b[1] + d[0] * d[0] + d[1] * d[1] + e * e
    cross = conj_cmul(a, b)
    cross = (cross[0] + c * d[0], cross[1] + c * d[1])
    ad = cmul(a, d)
    minor = (ad[0] - b[0] * c, ad[1] - b[1] * c)
    determinant = (
        minor[0] * minor[0]
        + minor[1] * minor[1]
        + (a[0] * a[0] + a[1] * a[1]) * e * e
        + c * c * e * e
    )
    first = (beta * a[0], -beta * a[1])
    second = (beta * b[0], -beta * b[1])
    t = cmul(cross, second)
    y0 = ((gram_second * first[0] - t[0]) / determinant, (gram_second * first[1] - t[1]) / determinant)
    t = conj_cmul(cross, first)
    y1 = ((gram_first * second[0] - t[0]) / determinant, (gram_first * second[1] - t[1]) / determinant)
    return y0, y1


def kernel(
    row_count,
    col_count,
    kept,
    forcing,
    medium,
    mask,
    source_rows,
    source_cols,
    refraction,
    mode_map,
    point_map,
    project_map,
    table_high,
    table_low,
    table_back,
    phases,
    solution_ref,
    residual_ref,
    fwd_high,
    fwd_low,
    phase,
    wave_ref,
    damp_ref,
    right_ref,
    rhs_cols,
    mixed,
    fixed,
    modes,
    high,
    low,
    send_feat,
    got_feat,
    all_feat,
    send_wave,
    got_wave,
    all_wave,
    got_scal,
    col_scal,
    ext,
    applied,
    basis,
    table_sems,
    halo_send,
    halo_recv,
    send_sems,
    recv_sems,
):
    lines, columns = mask.shape
    channels = mode_map.shape[2]
    groups = lines // LINES
    double = 2 * kept
    row = lax.axis_index("row")
    col = lax.axis_index("col")
    grid_scale = math.sqrt(lines * col_count * columns * row_count)

    table_copies = [
        pltpu.make_async_copy(table_high, fwd_high, table_sems.at[0]),
        pltpu.make_async_copy(table_low, fwd_low, table_sems.at[1]),
        pltpu.make_async_copy(phases.at[row], phase, table_sems.at[2]),
    ]
    back_copies = [
        pltpu.make_async_copy(table_back, rhs_cols.at[g, pl.ds(0, double)], table_sems.at[3 + g])
        for g in range(groups)
    ]
    for copy in table_copies + back_copies:
        copy.start()

    barrier = pltpu.get_barrier_semaphore()
    greeted = 0
    for d in range(1, row_count):
        pl.semaphore_signal(
            barrier, inc=1, device_id={"row": lax.rem(row + d, row_count)}, device_id_type=MESH
        )
        greeted += 1
    for d in range(1, col_count):
        pl.semaphore_signal(
            barrier, inc=1, device_id={"col": lax.rem(col + d, col_count)}, device_id_type=MESH
        )
        greeted += 1
    for dr in (1, row_count - 1):
        for dc in (1, col_count - 1):
            pl.semaphore_signal(
                barrier,
                inc=1,
                device_id={
                    "row": lax.rem(row + dr, row_count),
                    "col": lax.rem(col + dc, col_count),
                },
                device_id_type=MESH,
            )
            greeted += 1

    def spread(source, target, index, axis, me, count):
        for d in range(1, count):
            there = lax.rem(me + d, count)
            pltpu.make_async_remote_copy(
                src_ref=source(there),
                dst_ref=target.at[me],
                send_sem=send_sems.at[index],
                recv_sem=recv_sems.at[index],
                device_id={axis: there},
                device_id_type=MESH,
            ).start()

    def arrived(target, index, count, sems):
        whole = target.at[pl.ds(0, count - 1)]
        pltpu.make_async_copy(whole, whole, sems.at[index]).wait()

    def forward(out):
        spectrum = (
            jnp.dot(high[...], fwd_high[...], preferred_element_type=F32)
            + jnp.dot(high[...], fwd_low[...], preferred_element_type=F32)
            + jnp.dot(low[...], fwd_high[...], preferred_element_type=F32)
        )
        cosine, sine = phase[0:1, :kept], phase[0:1, kept:]
        re, im = spectrum[:, :kept], spectrum[:, kept:]
        out[:, :, 0:kept] = (re * cosine + im * sine).reshape(row_count, 8, kept)
        out[:, :, kept:double] = (im * cosine - re * sine).reshape(row_count, 8, kept)

    def unrotated(both):
        cosine, sine = phase[0:1, :kept], phase[0:1, kept:]
        re, im = both[:, :kept], both[:, kept:]
        return re * cosine - im * sine, im * cosine + re * sine

    def slab(g, j, value):
        rhs_cols[g, double + LINES * j : double + LINES * (j + 1), :] = value

    def field_slabs(g, j, value):
        top, rest = split(value)
        slab(g, j, top)
        slab(g, j + 1, rest)
        slab(g, j + 2, top)
        return top, rest

    def rows_of(g):
        return slice(LINES * g, LINES * (g + 1))

    def folded(x):
        total = jnp.zeros((8, 128), F32)
        for i in range(x.shape[0] // 8):
            for j in range(x.shape[1] // 128):
                total = total + x[8 * i : 8 * i + 8, 128 * j : 128 * j + 128]
        return total

    def scalar_tile(parts):
        place = lax.broadcasted_iota(jnp.int32, (8, 128), 0)
        tile = jnp.zeros((8, 128), F32)
        for i, part in enumerate(parts):
            tile = jnp.where(place == i, jnp.sum(part, axis=0, keepdims=True), tile)
        return tile

    for g in range(groups):
        lines_of = rows_of(g)
        kind = medium[lines_of, :]
        refractive = jnp.zeros((LINES, columns), F32)
        for level in range(refraction.shape[0]):
            refractive = jnp.where(kind == level, refraction[level], refractive)
        damping = 0.1 + mask[lines_of, :].astype(F32)
        damp_ref[lines_of, :] = damping
        scaled = wave_base * refractive
        wave_ref[lines_of, :] = scaled * scaled
        top, rest = field_slabs(g, 6, refractive)
        high[lines_of, :] = top
        low[lines_of, :] = rest
        top, rest = field_slabs(g, 9, damping)
        high[lines + LINES * g : lines + LINES * (g + 1), :] = top
        low[lines + LINES * g : lines + LINES * (g + 1), :] = rest
        ones = jnp.ones((LINES, columns), BF16)
        slab(g, 12, ones)
        slab(g, 13, ones)
        slab(g, 14, jnp.zeros_like(ones))
        slab(g, 15, jnp.zeros_like(ones))
    for copy in table_copies:
        copy.wait()
    forward(send_feat)
    pl.semaphore_wait(barrier, greeted)
    spread(lambda there: send_feat.at[there], got_feat, 0, "row", row, row_count)

    col_hits = (
        source_cols[...]
        == columns * row + lax.broadcasted_iota(jnp.int32, (source_cols.shape[0], columns), 1)
    ).astype(F32).astype(BF16)
    line_hits = (
        source_rows[...]
        == lines * col + lax.broadcasted_iota(jnp.int32, (lines, source_rows.shape[1]), 0)
    ).astype(F32).astype(BF16)
    source_count = jnp.dot(line_hits, col_hits, preferred_element_type=F32)
    square = jnp.zeros((8, 128), F32)
    for g in range(groups):
        lines_of = rows_of(g)
        for p in range(2):
            field = forcing[p, lines_of, :]
            if p == 0:
                field = field + source_gain * source_count[lines_of, :]
            right_ref[p, lines_of, :] = field
            square = square + folded(field * field)
            top, rest = split(field)
            high[p * lines + LINES * g : p * lines + LINES * (g + 1), :] = top
            low[p * lines + LINES * g : p * lines + LINES * (g + 1), :] = rest
    def send_modes(step, tile):
        forward(send_wave.at[step])
        for r in range(row_count):
            send_wave[step, r, :, double:] = tile
        spread(
            lambda there: send_wave.at[step, there], got_wave.at[step], 2 + 3 * step, "row", row, row_count
        )

    send_modes(0, scalar_tile([square]))

    for line in range(lines):
        i = line % LINES
        mixed[line, :, double:] = point_map[channels * i : channels * (i + 1), :]

    def reduced(got, source):
        got[row] = source[row]
        total = got[0]
        for r in range(1, row_count):
            total = total + got[r]
        return total

    arrived(got_feat, 0, row_count, recv_sems)
    all_feat[row] = reduced(got_feat, send_feat)
    spread(lambda there: all_feat.at[row], all_feat, 1, "row", row, row_count)

    def wave_reduce(step):
        index = 2 + 3 * step
        arrived(got_wave.at[step], index, row_count, recv_sems)
        total = reduced(got_wave.at[step], send_wave.at[step])
        all_wave[step, row] = total[:, :double]
        spread(
            lambda there: all_wave.at[step, row], all_wave.at[step], index + 1, "row", row, row_count
        )
        col_scal[step, col] = total[:, double:]
        spread(
            lambda there: col_scal.at[step, col], col_scal.at[step], index + 2, "col", col, col_count
        )

    def col_total(step):
        arrived(col_scal.at[step], 4 + 3 * step, col_count, recv_sems)
        total = col_scal[step, 0]
        for r in range(1, col_count):
            total = total + col_scal[step, r]
        return jnp.sum(total, axis=1, keepdims=True)

    def mix(channels_in, bias, source, store):
        for kc in range(kept // 128):
            low_k, high_k = pl.ds(128 * kc, 128), pl.ds(kept + 128 * kc, 128)
            for ob in range(channels // 16):
                outs = pl.ds(16 * ob, 16)
                maps = [
                    (mode_map[0, g, outs, low_k], mode_map[1, g, outs, low_k]) for g in channels_in
                ]
                start = (mode_map[0, 4, outs, low_k], mode_map[1, 4, outs, low_k]) if bias else None

                def eight_lines(block, carry):
                    first = pl.multiple_of(8 * block, 8)
                    parts = [
                        (modes[g, pl.ds(first, 8), low_k], modes[g, pl.ds(first, 8), high_k])
                        for g in channels_in
                    ]
                    for i in range(8):
                        line = first + i
                        if bias:
                            re, im = start
                        else:
                            re, im = source[line, outs, low_k], source[line, outs, high_k]
                        for (mode_re, mode_im), (map_re, map_im) in zip(parts, maps):
                            one_re, one_im = mode_re[i : i + 1], mode_im[i : i + 1]
                            re = re + (map_re * one_re - map_im * one_im)
                            im = im + (map_re * one_im + map_im * one_re)
                        store[line, outs, low_k] = re.astype(store.dtype)
                        store[line, outs, high_k] = im.astype(store.dtype)
                    return carry

                lax.fori_loop(0, lines // 8, eight_lines, 0)

    def layer(step):
        def one_group(g, carry):
            left = mixed[pl.ds(LINES * g, LINES)].reshape(LINES * channels, double + SLABS * LINES)
            first = pl.multiple_of(8 + LINES * g, 8)
            for n in range(columns // PIECE):
                piece = slice(PIECE * n, PIECE * (n + 1))
                x = jnp.dot(left, rhs_cols[g, :, piece], preferred_element_type=F32)
                active = gelu(x).astype(BF16)
                out = jnp.dot(project_map[...], active, preferred_element_type=F32)
                place = slice(128 + PIECE * n, 128 + PIECE * (n + 1))
                ext[step, 0, pl.ds(first, LINES), place] = out[:LINES]
                ext[step, 1, pl.ds(first, LINES), place] = out[LINES:]
            return carry

        lax.fori_loop(0, groups, one_group, 0)

    def halos(step):
        tall, wide = pl.ds(8, lines), pl.ds(128, columns)
        line_ends = {1: (pl.ds(lines, 8), pl.ds(0, 8)), -1: (pl.ds(8, 8), pl.ds(8 + lines, 8)), 0: (tall, tall)}
        col_ends = {
            1: (pl.ds(columns, 128), pl.ds(0, 128)),
            -1: (pl.ds(128, 128), pl.ds(128 + columns, 128)),
            0: (wide, wide),
        }
        copies = []
        for i, (dr, dc) in enumerate(
            [(1, 0), (-1, 0), (0, 1), (0, -1), (1, 1), (1, -1), (-1, 1), (-1, -1)]
        ):
            here_l, there_l = line_ends[dc]
            here_c, there_c = col_ends[dr]
            copies.append(
                pltpu.make_async_remote_copy(
                    src_ref=ext.at[step, :, here_l, here_c],
                    dst_ref=ext.at[step, :, there_l, there_c],
                    send_sem=halo_send.at[step, i],
                    recv_sem=halo_recv.at[step, i],
                    device_id={
                        "row": lax.rem(row + dr + row_count, row_count),
                        "col": lax.rem(col + dc + col_count, col_count),
                    },
                    device_id_type=MESH,
                )
            )
        for copy in copies:
            copy.start()
        for copy in copies:
            copy.wait()
        view = ext.at[step]

        @pl.when(row == 0)
        def _():
            view[:, :, 0:128] = jnp.zeros((2, lines + 16, 128), F32)

        @pl.when(row == row_count - 1)
        def _():
            view[:, :, 128 + columns :] = jnp.zeros((2, lines + 16, 128), F32)

        @pl.when(col == 0)
        def _():
            view[:, 0:8, :] = jnp.zeros((2, 8, columns + 256), F32)

        @pl.when(col == col_count - 1)
        def _():
            view[:, 8 + lines :, :] = jnp.zeros((2, 8, columns + 256), F32)

    def operate(step, g):
        laps, fields = [], []
        for p in range(2):
            first = 8 + LINES * g
            beside = (
                ext[step, p, first - 1 : first - 1 + LINES, :]
                + ext[step, p, first + 1 : first + 1 + LINES, :]
            )
            centre = ext[step, p, first : first + LINES, :]
            both = 4.0 * centre + beside
            width = columns + 256
            around = pltpu.roll(both, 1, 1) + pltpu.roll(both, width - 1, 1)
            total = (4.0 * beside - 20.0 * centre + around) * (1.0 / 6.0)
            laps.append(total[:, 128 : 128 + columns])
            fields.append(centre[:, 128 : 128 + columns])
        wave, damping = wave_ref[rows_of(g), :], damp_ref[rows_of(g), :]
        real = -laps[0] - wave * (fields[0] + damping * fields[1])
        imag = -laps[1] - wave * (fields[1] - damping * fields[0])
        return real, imag

    def pair(first, second):
        return (
            folded(first[0] * second[0] + first[1] * second[1]),
            folded(first[0] * second[1] - first[1] * second[0]),
        )

    def add(a, b):
        return [x + y for x, y in zip(a, b)]

    wave_reduce(0)
    arrived(all_feat, 1, row_count, recv_sems)
    re, im = unrotated(all_feat[...].reshape(2 * lines, double))
    for g in range(2):
        modes[2 + g, :, :kept] = re[g * lines : (g + 1) * lines]
        modes[2 + g, :, kept:] = im[g * lines : (g + 1) * lines]
    mix((2, 3), True, None, fixed)
    for copy in back_copies:
        copy.wait()

    arrived(all_wave.at[0], 3, row_count, recv_sems)
    total_square = col_total(0)[0:1, :]
    beta = jnp.sqrt(total_square + norm_eps)
    inverse_beta = 1.0 / beta
    re, im = unrotated(all_wave[0].reshape(2 * lines, double))
    for p in range(2):
        modes[p, :, :kept] = re[p * lines : (p + 1) * lines] * (grid_scale * inverse_beta)
        modes[p, :, kept:] = im[p * lines : (p + 1) * lines] * (grid_scale * inverse_beta)
    for g in range(groups):
        for p in range(2):
            field_slabs(g, 3 * p, right_ref[p, rows_of(g), :] * (grid_scale * inverse_beta))
    mix((0, 1), False, fixed, mixed)
    layer(0)
    halos(0)
    sums = [jnp.zeros((8, 128), F32)] * 3
    for g in range(groups):
        lines_of = rows_of(g)
        result = operate(0, g)
        for p in range(2):
            applied[0, p, lines_of, :] = result[p]
            top, rest = split(result[p])
            high[p * lines + LINES * g : p * lines + LINES * (g + 1), :] = top
            low[p * lines + LINES * g : p * lines + LINES * (g + 1), :] = rest
        start = (right_ref[0, lines_of, :], right_ref[1, lines_of, :])
        square = folded(result[0] * result[0] + result[1] * result[1])
        sums = add(sums, (*pair(start, result), square))
    send_modes(1, scalar_tile(sums))
    wave_reduce(1)
    arrived(all_wave.at[1], 6, row_count, recv_sems)
    totals = col_total(1)
    unit_square = total_square * inverse_beta * inverse_beta
    a = (totals[0:1, :] * inverse_beta, totals[1:2, :] * inverse_beta)
    a_square = a[0] * a[0] + a[1] * a[1]
    rest_square = jnp.maximum(totals[2:3, :] - a_square * (2.0 - unit_square), 0.0)
    c = jnp.sqrt(rest_square + norm_eps)
    inverse_c = 1.0 / c
    a_over = (a[0] * inverse_beta, a[1] * inverse_beta)

    def next_vector(w, v):
        scaled = cmul(a_over, v)
        return (w[0] - scaled[0]) * inverse_c, (w[1] - scaled[1]) * inverse_c

    old, new = (all_wave[i].reshape(2 * lines, double) for i in range(2))
    planes = next_vector((new[:lines], new[lines:]), (old[:lines], old[lines:]))
    for p in range(2):
        re, im = unrotated(planes[p])
        modes[p, :, :kept] = re * grid_scale
        modes[p, :, kept:] = im * grid_scale
    for g in range(groups):
        lines_of = rows_of(g)
        vector = next_vector(
            (applied[0, 0, lines_of, :], applied[0, 1, lines_of, :]),
            (right_ref[0, lines_of, :], right_ref[1, lines_of, :]),
        )
        for p in range(2):
            basis[p, lines_of, :] = vector[p]
            field_slabs(g, 3 * p, vector[p] * grid_scale)
    mix((0, 1), False, fixed, mixed)
    layer(1)
    halos(1)
    sums = [jnp.zeros((8, 128), F32)] * 5
    for g in range(groups):
        lines_of = rows_of(g)
        result = operate(1, g)
        for p in range(2):
            applied[1, p, lines_of, :] = result[p]
        start = (right_ref[0, lines_of, :], right_ref[1, lines_of, :])
        vector = (basis[0, lines_of, :], basis[1, lines_of, :])
        square = folded(result[0] * result[0] + result[1] * result[1])
        sums = add(sums, (*pair(start, result), *pair(vector, result), square))
    got_scal[row] = scalar_tile(sums)
    spread(lambda there: got_scal.at[row], got_scal, 8, "row", row, row_count)
    arrived(got_scal, 8, row_count, recv_sems)
    total = got_scal[0]
    for r in range(1, row_count):
        total = total + got_scal[r]
    col_scal[2, col] = total
    spread(lambda there: col_scal.at[2, col], col_scal.at[2], 9, "col", col, col_count)
    arrived(col_scal.at[2], 9, col_count, recv_sems)
    total = col_scal[2, 0]
    for r in range(1, col_count):
        total = total + col_scal[2, r]
    totals = jnp.sum(total, axis=1, keepdims=True)
    b = (totals[0:1, :] * inverse_beta, totals[1:2, :] * inverse_beta)
    d = (totals[2:3, :], totals[3:4, :])
    b_square = b[0] * b[0] + b[1] * b[1]
    d_square = d[0] * d[0] + d[1] * d[1]
    second_square = rest_square * inverse_c * inverse_c
    overlap = (norm_eps * inverse_beta * inverse_beta) * inverse_c
    between = conj_cmul(b, d)
    between = between[0] * a[0] - between[1] * a[1]
    last_square = (
        totals[4:5, :]
        - b_square * (2.0 - unit_square)
        - d_square * (2.0 - second_square)
        + 2.0 * overlap * between
    )
    e = jnp.sqrt(jnp.maximum(last_square, 0.0) + norm_eps)
    y0, y1 = small_solve(beta, a, b, c, d, e)
    for g in range(groups):
        lines_of = rows_of(g)
        inner = slice(8 + LINES * g, 8 + LINES * (g + 1))
        z0, z1, w0, w1 = (
            [ext[0, p, inner, 128 : 128 + columns] for p in range(2)],
            [ext[1, p, inner, 128 : 128 + columns] for p in range(2)],
            [applied[0, p, lines_of, :] for p in range(2)],
            [applied[1, p, lines_of, :] for p in range(2)],
        )
        z0, z1, w0, w1 = cmul(y0, z0), cmul(y1, z1), cmul(y0, w0), cmul(y1, w1)
        for p in range(2):
            solution_ref[p, lines_of, :] = z0[p] + z1[p]
            residual_ref[p, lines_of, :] = right_ref[p, lines_of, :] - w0[p] - w1[p]

    arrived(got_feat, 0, row_count, send_sems)
    arrived(all_feat, 1, row_count, send_sems)
    for step in range(2):
        arrived(got_wave.at[step], 2 + 3 * step, row_count, send_sems)
        arrived(all_wave.at[step], 3 + 3 * step, row_count, send_sems)
        arrived(col_scal.at[step], 4 + 3 * step, col_count, send_sems)
    arrived(got_scal, 8, row_count, send_sems)
    arrived(col_scal.at[2], 9, col_count, send_sems)


def rounded(x):
    return lax.reduce_precision(x, 8, 7)


def shards(
    row_count,
    col_count,
    kept,
    forcing,
    medium_index,
    absorbing_mask,
    source_rows,
    source_cols,
    refraction,
    lift_weight,
    lift_bias,
    spectral_weight,
    point_weight,
    layer_bias,
    project_weight,
):
    _, lines, columns = forcing.shape
    channels = point_weight.shape[0]
    grid_cols = columns * row_count
    groups = lines // LINES
    double = 2 * kept
    assert row_count * 8 == 2 * lines

    table_high, table_low, table_back = base_tables(columns, kept, grid_cols)
    phases = phase_table(row_count, kept)

    highest = lax.Precision.HIGHEST
    lift = jnp.concatenate([lift_weight, lift_bias[None]], axis=0)
    mode_map = jnp.einsum("gc,pkco->pgok", lift, spectral_weight.astype(F32), precision=highest)
    twice = np.where(np.arange(kept) == 0, 1.0, 2.0).astype(np.float32)
    anchor = np.where(np.arange(kept) == 0, math.sqrt(grid_cols), 0.0).astype(np.float32)
    mode_map = mode_map * jnp.stack([twice] * 4 + [anchor])[None, :, None, :]

    point = jnp.einsum("co,gc->og", point_weight.astype(F32), lift, precision=highest)
    point = point + jnp.where(jnp.arange(5) == 4, layer_bias[:, None], 0.0)
    top = rounded(point)
    rest = rounded(point - top)
    order = []
    for g in range(4):
        order += [top[:, g], top[:, g], rest[:, g]]
    order += [top[:, 4], rest[:, 4], jnp.zeros_like(top[:, 4]), jnp.zeros_like(top[:, 4])]
    one_line = jnp.stack(order, axis=1)
    eye = jnp.eye(LINES, dtype=F32)
    point_map = (one_line[None, :, :, None] * eye[:, None, None, :]).reshape(
        LINES * channels, SLABS * LINES
    ).astype(BF16)
    project_map = (
        project_weight.astype(F32).T[:, None, None, :] * eye[None, :, :, None]
    ).reshape(2 * LINES, LINES * channels).astype(BF16)

    field = jax.ShapeDtypeStruct((2, lines, columns), F32)
    vmem = pl.BlockSpec(memory_space=pltpu.VMEM)
    smem = pl.BlockSpec(memory_space=pltpu.SMEM)
    hbm = pl.BlockSpec(memory_space=pl.ANY)
    dma = pltpu.SemaphoreType.DMA
    return pl.pallas_call(
        functools.partial(kernel, row_count, col_count, kept),
        out_shape=(field, field),
        in_specs=[vmem] * 5 + [smem] + [vmem] * 3 + [hbm] * 4,
        out_specs=(vmem, vmem),
        scratch_shapes=[
            pltpu.VMEM((columns, double), BF16),
            pltpu.VMEM((columns, double), BF16),
            pltpu.VMEM((8, double), F32),
            pltpu.VMEM((lines, columns), F32),
            pltpu.VMEM((lines, columns), F32),
            pltpu.VMEM((2, lines, columns), F32),
            pltpu.VMEM((groups, double + SLABS * LINES, columns), BF16),
            pltpu.VMEM((lines, channels, double + SLABS * LINES), BF16),
            pltpu.VMEM((lines, channels, double), F32),
            pltpu.VMEM((4, lines, double), F32),
            pltpu.VMEM((2 * lines, columns), BF16),
            pltpu.VMEM((2 * lines, columns), BF16),
            pltpu.VMEM((row_count, 8, double), F32),
            pltpu.VMEM((row_count, 8, double), F32),
            pltpu.VMEM((row_count, 8, double), F32),
            pltpu.VMEM((2, row_count, 8, double + 128), F32),
            pltpu.VMEM((2, row_count, 8, double + 128), F32),
            pltpu.VMEM((2, row_count, 8, double), F32),
            pltpu.VMEM((row_count, 8, 128), F32),
            pltpu.VMEM((3, col_count, 8, 128), F32),
            pltpu.VMEM((2, 2, lines + 16, columns + 256), F32),
            pltpu.VMEM((2, 2, lines, columns), F32),
            pltpu.VMEM((2, lines, columns), F32),
            dma((3 + groups,)),
            dma((2, 8)),
            dma((2, 8)),
            dma((10,)),
            dma((10,)),
        ],
        compiler_params=pltpu.CompilerParams(
            collective_id=0, has_side_effects=True, vmem_limit_bytes=56 * 2**20
        ),
        name="krylov",
    )(
        forcing,
        medium_index,
        absorbing_mask,
        source_rows.reshape(1, -1),
        source_cols.reshape(-1, 1),
        refraction,
        mode_map,
        point_map,
        project_map,
        table_high,
        table_low,
        table_back,
        phases,
    )


def solution(mesh):
    return jax.shard_map(
        functools.partial(shards, mesh.shape["row"], mesh.shape["col"], K),
        mesh=mesh,
        in_specs=(
            P(None, "col", "row"),
            P("col", "row"),
            P("col", "row"),
            P(),
            P(),
            P(),
            P(),
            P(),
            P(),
            P(),
            P(),
            P(),
        ),
        out_specs=(P(None, "col", "row"), P(None, "col", "row")),
        check_vma=False,
    )
```

time: 1140 us -> 119 us (0.10)
  blocking collectives: 434 us -> 0 us
  local copies, waits for them, and re-layouts: 218 us -> 7.77 us
  matrix products: 215 us -> 7.16 us
  other arithmetic: 190 us -> 2.11 us
  Pallas kernels: 0 us -> 101 us
  starting transfers between devices: 36.4 us -> 0 us
  between operations: 34.6 us -> 0.72 us
    psum x6 -> x0, blocking collectives: 390 us -> none  [the longest x3 195 us: squared_total(): return lax.psum(jnp.sum(grid_field * grid_field), ('row', 'col'))]
    dot_general x18 -> x2, matrix products: 215 us -> 7.16 us  [the longest x1 6.35 us: shards(): jnp.einsum('gc,pkco->pgok', lift, spectral_weight.astype(F32), precision=...]
    unnamed x89 -> x6, local copies, waits for them, and re-layouts: 135 us -> 3.82 us
    pallas_call x0 -> x1, Pallas kernels: none -> 101 us  [shards(): pl.pallas_call(functools.partial(kernel, row_count, col_count, kept), out...]
    another operation x3 -> x0, other arithmetic: 73.8 us -> none
    mul x6 -> x1, other arithmetic: 70.2 us -> 1.05 us  [shards(): mode_map = mode_map * jnp.stack([twice] * 4 + [anchor])[None, :, None, :]]
    all_to_all x3 -> x0, blocking collectives: 43.9 us -> none  [the longest x2 29.3 us: shards(): lax.all_to_all(line_result, 'row', split_axis=2, concat_axis=1, tiled=True)]
    all_to_all x10 -> x0, local copies, waits for them, and re-layouts: 29.3 us -> none  [the longest x7 28.4 us: shards(): lax.all_to_all(line_result, 'row', split_axis=2, concat_axis=1, tiled=True)]
  transfers between devices with their start and end apart: 10 -> 0, of which waited for: 1 -> 0; matrix products, arithmetic and copies ran while one was open for 16% -> 0% of each run, Pallas kernels for 0% -> 0%
where the time goes in v1:
time: 119 us; the launch traced here: 118 us
  Pallas kernels  101 us (85%)
  local copies, waits for them, and re-layouts  7.77 us (7%)
  matrix products  7.16 us (6%)
  other arithmetic  2.11 us (2%)
    pallas_call x1, Pallas kernels, shards(): pl.pallas_call(functools.partial(kernel, row_count, col_count, kept), out...  101 us
    dot_general x1, matrix products, shards(): jnp.einsum('gc,pkco->pgok', lift, spectral_weight.astype(F32), precision=...  6.35 us
    unnamed x6, local copies, waits for them, and re-layouts  3.82 us

profile of v1, /device:TPU:1, one launch (start us, length us, event | category | flops | bytes accessed | tf_op | source)
XLA Modules:
  0.0 118.3 jit_solution(17038331585875067297)
XLA Ops:
  0.6 0.0 copy-start
  0.7 0.7 convert_bitcast_fusion
  1.3 0.0 copy-done
  1.4 0.8 subtract_reduce-precision_fusion
  2.2 0.1 stack.31
  2.3 0.1 copy.42
  2.3 1.3 %copy.43.source_cols = s32[16,1]{1,0:T(8,128)} copy(s32[16,1]{0,1:T(1,128)} %bitcast.26) | data formatting | bytes 128 | tf_op jit(solution)/shard_map/reshape | solution.py:693
  3.7 0.1 multiply_convert_fusion.1
  3.8 0.8 convert_element_type.30.project_map
  4.5 0.3 multiply_convert_fusion
  4.8 0.0 copy-start.1
  4.8 0.7 convert_element_type.28
  5.6 1.0 copy.44.point_map
  6.6 6.4 %fusion = f32[5,2,256,64]{2,0,3,1:T(8,128)S(1)} fusion(bf16[2,256,64,64]{1,3,2,0:T(8,128)(2,1)} %param.29, f32[1,64]{1,0:T(1,128)} %bitcast.24, f32[4,64]{1,0:T(4,128)} %param.27), kind=kOutput, calls=%fused_computation | convolution fusion | flops 125829440 | bytes 4850944 | tf_op jit(solution)/shard_map/gc,pkco->pgok/dot_general | solution.py:622
  12.9 0.0 copy-done.1
  12.9 1.1 fusion.3.mode_map
  14.0 100.6 %krylov.1 = (f32[2,64,1024]{2,1,0:T(8,128)}, f32[2,64,1024]{2,1,0:T(8,128)}) custom-call(f32[2,64,1024]{2,1,0:T(8,128)} %forcing.1, s32[64,1024]{1,0:T(8,128)} %medium.1, s32[64,1024]{1,0:T(8,128)} %mask.1, s32[1,16]{1,0:T(1,128)} %bitcast.25, s32[16,1]{1,0:T(8,128)} %copy.43.source_cols, f32[8]{0:T(128)} %refraction.1, f32[2,5,64,256]{3,2,1,0:T(8,128)} %fusion.3.mode_map, ...), custom_call_target="tpu_custom_call" | custom-call | tf_op jit(solution)/shard_map/krylov/pallas_call | solution.py:649
  114.6 1.9 %copy.53 = f32[2,64,1024]{2,1,0:T(8,128)} copy(f32[2,64,1024]{2,1,0:T(8,128)} %get-tuple-element.22) | data formatting | bytes 1048576
  116.4 1.9 %copy.54 = f32[2,64,1024]{2,1,0:T(8,128)} copy(f32[2,64,1024]{2,1,0:T(8,128)} %get-tuple-element.23) | data formatting | bytes 1048576
  (4 shorter events, 0.0 us)
Async XLA Ops:
  0.6 0.7 copy-start
  4.8 8.1 %copy-start.1 = (f32[5,256]{1,0:T(8,128)S(1)}, f32[5,256]{1,0:T(8,128)}, u32[]{:S(2)}) copy-start(f32[5,256]{1,0:T(8,128)} %constant.25) | copy-start | bytes 15364

commit v2 on v1

--- a/solution.py
+++ b/solution.py
@@ -46,6 +46,11 @@
 def split(x):
     high = x.astype(BF16)
     return high, (x - high.astype(F32)).astype(BF16)
+
+
+def three_way(x):
+    high, low = split(x)
+    return high, low, (x - high.astype(F32) - low.astype(F32)).astype(BF16)
 
 
 def gelu(x):
@@ -92,9 +97,12 @@
     source_rows,
     source_cols,
     refraction,
-    mode_map,
-    point_map,
-    project_map,
+    lift_weight,
+    lift_bias,
+    spectral_weight,
+    point_weight,
+    layer_bias,
+    project_weight,
     table_high,
     table_low,
     table_back,
@@ -104,6 +112,10 @@
     fwd_high,
     fwd_low,
     phase,
+    weights,
+    by_mode,
+    mode_map,
+    project_map,
     wave_ref,
     damp_ref,
     right_ref,
@@ -121,6 +133,7 @@
     all_wave,
     got_scal,
     col_scal,
+    before,
     ext,
     applied,
     basis,
@@ -131,7 +144,7 @@
     recv_sems,
 ):
     lines, columns = mask.shape
-    channels = mode_map.shape[2]
+    channels = point_weight.shape[0]
     groups = lines // LINES
     double = 2 * kept
     row = lax.axis_index("row")
@@ -147,7 +160,8 @@
         pltpu.make_async_copy(table_back, rhs_cols.at[g, pl.ds(0, double)], table_sems.at[3 + g])
         for g in range(groups)
     ]
-    for copy in table_copies + back_copies:
+    weight_copy = pltpu.make_async_copy(spectral_weight, weights, table_sems.at[3 + groups])
+    for copy in [*table_copies, weight_copy, *back_copies]:
         copy.start()
 
     barrier = pltpu.get_barrier_semaphore()
@@ -261,14 +275,22 @@
     pl.semaphore_wait(barrier, greeted)
     spread(lambda there: send_feat.at[there], got_feat, 0, "row", row, row_count)
 
-    col_hits = (
-        source_cols[...]
-        == columns * row + lax.broadcasted_iota(jnp.int32, (source_cols.shape[0], columns), 1)
-    ).astype(F32).astype(BF16)
-    line_hits = (
-        source_rows[...]
-        == lines * col + lax.broadcasted_iota(jnp.int32, (lines, source_rows.shape[1]), 0)
-    ).astype(F32).astype(BF16)
+    sources = source_rows.shape[0]
+    place = lax.broadcasted_iota(jnp.int32, (sources, 128), 0)
+    col_of = jnp.zeros((sources, 128), jnp.int32)
+    for i in range(sources):
+        col_of = jnp.where(place == i, source_cols[i] - columns * row, col_of)
+    lane = lax.broadcasted_iota(jnp.int32, (sources, 128), 1)
+    col_hits = jnp.concatenate(
+        [jnp.where(col_of == lane + 128 * j, 1.0, 0.0) for j in range(columns // 128)], axis=1
+    ).astype(BF16)
+    place = lax.broadcasted_iota(jnp.int32, (lines, sources), 1)
+    row_of = jnp.zeros((lines, sources), jnp.int32)
+    for i in range(sources):
+        row_of = jnp.where(place == i, source_rows[i] - lines * col, row_of)
+    line_hits = jnp.where(
+        row_of == lax.broadcasted_iota(jnp.int32, (lines, sources), 0), 1.0, 0.0
+    ).astype(BF16)
     source_count = jnp.dot(line_hits, col_hits, preferred_element_type=F32)
     square = jnp.zeros((8, 128), F32)
     for g in range(groups):
@@ -292,9 +314,81 @@
 
     send_modes(0, scalar_tile([square]))
 
-    for line in range(lines):
-        i = line % LINES
-        mixed[line, :, double:] = point_map[channels * i : channels * (i + 1), :]
+    lift = jnp.concatenate(
+        [lift_weight[...], lift_bias[...], jnp.zeros((3, channels), F32)], axis=0
+    )
+    lift_parts = three_way(lift)
+    point = jnp.zeros((8, channels), F32)
+    for part in lift_parts:
+        point = point + jnp.dot(part, point_weight[...], preferred_element_type=F32)
+    channel_row = lax.broadcasted_iota(jnp.int32, (8, channels), 0)
+    point = point + jnp.where(channel_row == 4, layer_bias[...], 0.0)
+    top, rest = split(point)
+    wide = SLABS * LINES
+    from_row = lax.broadcasted_iota(jnp.int32, (8, wide), 0)
+    slab_of = lax.broadcasted_iota(jnp.int32, (8, wide), 1) // LINES
+    first_slab = 3 * from_row
+    pick_top = ((slab_of == first_slab) | ((slab_of == first_slab + 1) & (from_row < 4))) & (from_row < 5)
+    pick_rest = ((slab_of == first_slab + 2) & (from_row < 4)) | ((slab_of == 13) & (from_row == 4))
+    over_rows = (((0,), (0,)), ((), ()))
+    spread_out = lax.dot_general(
+        top.astype(F32), jnp.where(pick_top, 1.0, 0.0), over_rows, preferred_element_type=F32
+    ) + lax.dot_general(
+        rest.astype(F32), jnp.where(pick_rest, 1.0, 0.0), over_rows, preferred_element_type=F32
+    )
+    line_of = lax.broadcasted_iota(jnp.int32, (channels, wide), 1) % LINES
+    for i in range(LINES):
+        masked = jnp.where(line_of == i, spread_out, 0.0).astype(BF16)
+        for g in range(groups):
+            mixed[LINES * g + i, :, double:] = masked
+    all_rows = LINES * channels
+    tiles = jnp.where(
+        lax.broadcasted_iota(jnp.int32, (channels, all_rows), 0)
+        == lax.broadcasted_iota(jnp.int32, (channels, all_rows), 1) % channels,
+        1.0,
+        0.0,
+    )
+    across = lax.dot_general(
+        project_weight[...].astype(F32), tiles, over_rows, preferred_element_type=F32
+    )
+    own_line = (
+        lax.broadcasted_iota(jnp.int32, (LINES, all_rows), 0)
+        == lax.broadcasted_iota(jnp.int32, (LINES, all_rows), 1) // channels
+    )
+    for p in range(2):
+        project_map[LINES * p : LINES * (p + 1), :] = jnp.where(
+            own_line, across[p : p + 1, :], 0.0
+        ).astype(BF16)
+
+    own_mode = (
+        lax.broadcasted_iota(jnp.int32, (8, 8 * channels), 0)
+        == lax.broadcasted_iota(jnp.int32, (8, 8 * channels), 1) // channels
+    )
+    stacked = []
+    for part in lift_parts[:2]:
+        along = jnp.concatenate([part.astype(F32)] * 8, axis=1)
+        stacked += [jnp.where(own_mode, along[g : g + 1, :], 0.0) for g in range(5)]
+    stacked = jnp.concatenate(stacked, axis=0).astype(BF16)
+    weight_copy.wait()
+
+    def eight_modes(block, carry):
+        first = pl.multiple_of(8 * block, 8)
+        for part in range(2):
+            some = weights[part, pl.ds(first, 8)].reshape(8 * channels, channels)
+            both = jnp.dot(stacked, some, preferred_element_type=F32)
+            both = both[:40] + both[40:]
+            for g in range(5):
+                by_mode[part, g, pl.ds(first, 8), 0:channels] = both[8 * g : 8 * g + 8]
+        return carry
+
+    lax.fori_loop(0, kept // 8, eight_modes, 0)
+    mode_of = lax.broadcasted_iota(jnp.int32, (1, kept), 1)
+    twice = jnp.where(mode_of == 0, 1.0, 2.0)
+    anchor = jnp.where(mode_of == 0, math.sqrt(columns * row_count), 0.0)
+    for part in range(2):
+        for g in range(5):
+            turned = jnp.transpose(by_mode[part, g])[:channels]
+            mode_map[part, g] = turned * (twice if g < 4 else anchor)
 
     def reduced(got, source):
         got[row] = source[row]
@@ -327,61 +421,94 @@
             total = total + col_scal[step, r]
         return jnp.sum(total, axis=1, keepdims=True)
 
-    def mix(channels_in, bias, source, store):
+    def mix_lines(first, count, kc, ob, channels_in, bias, source, store):
+        low_k, high_k = pl.ds(128 * kc, 128), pl.ds(kept + 128 * kc, 128)
+        outs = pl.ds(16 * ob, 16)
+        maps = [(mode_map[0, g, outs, low_k], mode_map[1, g, outs, low_k]) for g in channels_in]
+        start = (mode_map[0, 4, outs, low_k], mode_map[1, 4, outs, low_k]) if bias else None
+        for block in range(count // 8):
+            top = first + 8 * block
+            parts = [
+                (modes[g, pl.ds(top, 8), low_k], modes[g, pl.ds(top, 8), high_k]) for g in channels_in
+            ]
+            for i in range(8):
+                line = top + i
+                if bias:
+                    re, im = start
+                else:
+                    re, im = source[line, outs, low_k], source[line, outs, high_k]
+                for (mode_re, mode_im), (map_re, map_im) in zip(parts, maps):
+                    one_re, one_im = mode_re[i : i + 1], mode_im[i : i + 1]
+                    re = re + (map_re * one_re - map_im * one_im)
+                    im = im + (map_re * one_im + map_im * one_re)
+                store[line, outs, low_k] = re.astype(store.dtype)
+                store[line, outs, high_k] = im.astype(store.dtype)
+
+    def mix_fixed():
         for kc in range(kept // 128):
-            low_k, high_k = pl.ds(128 * kc, 128), pl.ds(kept + 128 * kc, 128)
             for ob in range(channels // 16):
-                outs = pl.ds(16 * ob, 16)
-                maps = [
-                    (mode_map[0, g, outs, low_k], mode_map[1, g, outs, low_k]) for g in channels_in
-                ]
-                start = (mode_map[0, 4, outs, low_k], mode_map[1, 4, outs, low_k]) if bias else None
 
                 def eight_lines(block, carry):
                     first = pl.multiple_of(8 * block, 8)
-                    parts = [
-                        (modes[g, pl.ds(first, 8), low_k], modes[g, pl.ds(first, 8), high_k])
-                        for g in channels_in
-                    ]
-                    for i in range(8):
-                        line = first + i
-                        if bias:
-                            re, im = start
-                        else:
-                            re, im = source[line, outs, low_k], source[line, outs, high_k]
-                        for (mode_re, mode_im), (map_re, map_im) in zip(parts, maps):
-                            one_re, one_im = mode_re[i : i + 1], mode_im[i : i + 1]
-                            re = re + (map_re * one_re - map_im * one_im)
-                            im = im + (map_re * one_im + map_im * one_re)
-                        store[line, outs, low_k] = re.astype(store.dtype)
-                        store[line, outs, high_k] = im.astype(store.dtype)
+                    mix_lines(first, 8, kc, ob, (2, 3), True, None, fixed)
                     return carry
 
                 lax.fori_loop(0, lines // 8, eight_lines, 0)
 
+    def mix_group(g):
+        for kc in range(kept // 128):
+            for ob in range(channels // 16):
+                mix_lines(LINES * g, LINES, kc, ob, (0, 1), False, fixed, mixed)
+
     def layer(step):
-        def one_group(g, carry):
-            left = mixed[pl.ds(LINES * g, LINES)].reshape(LINES * channels, double + SLABS * LINES)
-            first = pl.multiple_of(8 + LINES * g, 8)
-            for n in range(columns // PIECE):
-                piece = slice(PIECE * n, PIECE * (n + 1))
-                x = jnp.dot(left, rhs_cols[g, :, piece], preferred_element_type=F32)
-                active = gelu(x).astype(BF16)
-                out = jnp.dot(project_map[...], active, preferred_element_type=F32)
-                place = slice(128 + PIECE * n, 128 + PIECE * (n + 1))
-                ext[step, 0, pl.ds(first, LINES), place] = out[:LINES]
-                ext[step, 1, pl.ds(first, LINES), place] = out[LINES:]
-            return carry
-
-        lax.fori_loop(0, groups, one_group, 0)
-
-    def halos(step):
-        tall, wide = pl.ds(8, lines), pl.ds(128, columns)
-        line_ends = {1: (pl.ds(lines, 8), pl.ds(0, 8)), -1: (pl.ds(8, 8), pl.ds(8 + lines, 8)), 0: (tall, tall)}
+        last = columns // PIECE - 1
+        edges = [(g, n) for g in range(groups) for n in sorted({0, last})]
+        ends = [(g, n) for g in sorted({0, groups - 1}) for n in range(1, last)]
+        inside = [(g, n) for g in range(1, groups - 1) for n in range(1, last)]
+        order = edges + ends + inside
+        copies = halo_copies(step)
+
+        def multiply(g, n, slot):
+            left = mixed[LINES * g : LINES * (g + 1)].reshape(LINES * channels, double + SLABS * LINES)
+            before[slot] = jnp.dot(
+                left, rhs_cols[g, :, PIECE * n : PIECE * (n + 1)], preferred_element_type=F32
+            )
+
+        def finish(g, n, slot):
+            active = gelu(before[slot]).astype(BF16)
+            out = jnp.dot(project_map[...], active, preferred_element_type=F32)
+            first = 8 + LINES * g
+            place = slice(128 + PIECE * n, 128 + PIECE * (n + 1))
+            ext[step, 0, first : first + LINES, place] = out[:LINES]
+            ext[step, 1, first : first + LINES, place] = out[LINES:]
+
+        mix_group(0)
+        for t in range(len(order) + 1):
+            if t < len(order):
+                g, n = order[t]
+                multiply(g, n, t % 2)
+                if t < len(edges) and n == 0 and g + 1 < groups:
+                    mix_group(g + 1)
+            if t > 0:
+                finish(*order[t - 1], (t - 1) % 2)
+            if t == len(edges):
+                for i in (0, 1, 4, 5, 6, 7):
+                    copies[i].start()
+            if t == len(edges) + len(ends):
+                for i in (2, 3):
+                    copies[i].start()
+
+    def halo_copies(step):
+        tall, across_all = pl.ds(8, lines), pl.ds(128, columns)
+        line_ends = {
+            1: (pl.ds(lines, 8), pl.ds(0, 8)),
+            -1: (pl.ds(8, 8), pl.ds(8 + lines, 8)),
+            0: (tall, tall),
+        }
         col_ends = {
             1: (pl.ds(columns, 128), pl.ds(0, 128)),
             -1: (pl.ds(128, 128), pl.ds(128 + columns, 128)),
-            0: (wide, wide),
+            0: (across_all, across_all),
         }
         copies = []
         for i, (dr, dc) in enumerate(
@@ -402,9 +529,10 @@
                     device_id_type=MESH,
                 )
             )
-        for copy in copies:
-            copy.start()
-        for copy in copies:
+        return copies
+
+    def halos(step):
+        for copy in halo_copies(step):
             copy.wait()
         view = ext.at[step]
 
@@ -459,7 +587,7 @@
     for g in range(2):
         modes[2 + g, :, :kept] = re[g * lines : (g + 1) * lines]
         modes[2 + g, :, kept:] = im[g * lines : (g + 1) * lines]
-    mix((2, 3), True, None, fixed)
+    mix_fixed()
     for copy in back_copies:
         copy.wait()
 
@@ -474,7 +602,6 @@
     for g in range(groups):
         for p in range(2):
             field_slabs(g, 3 * p, right_ref[p, rows_of(g), :] * (grid_scale * inverse_beta))
-    mix((0, 1), False, fixed, mixed)
     layer(0)
     halos(0)
     sums = [jnp.zeros((8, 128), F32)] * 3
@@ -520,7 +647,6 @@
         for p in range(2):
             basis[p, lines_of, :] = vector[p]
             field_slabs(g, 3 * p, vector[p] * grid_scale)
-    mix((0, 1), False, fixed, mixed)
     layer(1)
     halos(1)
     sums = [jnp.zeros((8, 128), F32)] * 5
@@ -586,10 +712,6 @@
     arrived(col_scal.at[2], 9, col_count, send_sems)
 
 
-def rounded(x):
-    return lax.reduce_precision(x, 8, 7)
-
-
 def shards(
     row_count,
     col_count,
@@ -617,30 +739,6 @@
     table_high, table_low, table_back = base_tables(columns, kept, grid_cols)
     phases = phase_table(row_count, kept)
 
-    highest = lax.Precision.HIGHEST
-    lift = jnp.concatenate([lift_weight, lift_bias[None]], axis=0)
-    mode_map = jnp.einsum("gc,pkco->pgok", lift, spectral_weight.astype(F32), precision=highest)
-    twice = np.where(np.arange(kept) == 0, 1.0, 2.0).astype(np.float32)
-    anchor = np.where(np.arange(kept) == 0, math.sqrt(grid_cols), 0.0).astype(np.float32)
-    mode_map = mode_map * jnp.stack([twice] * 4 + [anchor])[None, :, None, :]
-
-    point = jnp.einsum("co,gc->og", point_weight.astype(F32), lift, precision=highest)
-    point = point + jnp.where(jnp.arange(5) == 4, layer_bias[:, None], 0.0)
-    top = rounded(point)
-    rest = rounded(point - top)
-    order = []
-    for g in range(4):
-        order += [top[:, g], top[:, g], rest[:, g]]
-    order += [top[:, 4], rest[:, 4], jnp.zeros_like(top[:, 4]), jnp.zeros_like(top[:, 4])]
-    one_line = jnp.stack(order, axis=1)
-    eye = jnp.eye(LINES, dtype=F32)
-    point_map = (one_line[None, :, :, None] * eye[:, None, None, :]).reshape(
-        LINES * channels, SLABS * LINES
-    ).astype(BF16)
-    project_map = (
-        project_weight.astype(F32).T[:, None, None, :] * eye[None, :, :, None]
-    ).reshape(2 * LINES, LINES * channels).astype(BF16)
-
     field = jax.ShapeDtypeStruct((2, lines, columns), F32)
     vmem = pl.BlockSpec(memory_space=pltpu.VMEM)
     smem = pl.BlockSpec(memory_space=pltpu.SMEM)
@@ -649,12 +747,16 @@
     return pl.pallas_call(
         functools.partial(kernel, row_count, col_count, kept),
         out_shape=(field, field),
-        in_specs=[vmem] * 5 + [smem] + [vmem] * 3 + [hbm] * 4,
+        in_specs=[vmem] * 3 + [smem] * 3 + [vmem] * 2 + [hbm] + [vmem] * 3 + [hbm] * 4,
         out_specs=(vmem, vmem),
         scratch_shapes=[
             pltpu.VMEM((columns, double), BF16),
             pltpu.VMEM((columns, double), BF16),
             pltpu.VMEM((8, double), F32),
+            pltpu.VMEM((2, kept, channels, channels), BF16),
+            pltpu.VMEM((2, 5, kept, 128), F32),
+            pltpu.VMEM((2, 5, channels, kept), F32),
+            pltpu.VMEM((2 * LINES, LINES * channels), BF16),
             pltpu.VMEM((lines, columns), F32),
             pltpu.VMEM((lines, columns), F32),
             pltpu.VMEM((2, lines, columns), F32),
@@ -672,10 +774,11 @@
             pltpu.VMEM((2, row_count, 8, double), F32),
             pltpu.VMEM((row_count, 8, 128), F32),
             pltpu.VMEM((3, col_count, 8, 128), F32),
+            pltpu.VMEM((2, LINES * channels, PIECE), F32),
             pltpu.VMEM((2, 2, lines + 16, columns + 256), F32),
             pltpu.VMEM((2, 2, lines, columns), F32),
             pltpu.VMEM((2, lines, columns), F32),
-            dma((3 + groups,)),
+            dma((4 + groups,)),
             dma((2, 8)),
             dma((2, 8)),
             dma((10,)),
@@ -689,12 +792,15 @@
         forcing,
         medium_index,
         absorbing_mask,
-        source_rows.reshape(1, -1),
-        source_cols.reshape(-1, 1),
+        source_rows,
+        source_cols,
         refraction,
-        mode_map,
-        point_map,
-        project_map,
+        lift_weight,
+        lift_bias.reshape(1, -1),
+        spectral_weight,
+        point_weight,
+        layer_bias.reshape(1, -1),
+        project_weight,
         table_high,
         table_low,
         table_back,

time: 119 us -> 95.7 us (0.80)
  Pallas kernels: 101 us -> 76.5 us
  local copies, waits for them, and re-layouts: 7.77 us -> 18.1 us
  matrix products: 7.16 us -> 0 us
  other arithmetic: 2.11 us -> 0 us
    pallas_call x1, Pallas kernels: 101 us -> 76.5 us  [shards(): pl.pallas_call(functools.partial(kernel, row_count, col_count, kept), out...]
    unnamed x6 -> x4, local copies, waits for them, and re-layouts: 3.82 us -> 18.1 us
    dot_general x2 -> x0, matrix products: 7.16 us -> none  [the longest x1 6.35 us: shards(): jnp.einsum('gc,pkco->pgok', lift, spectral_weight.astype(F32), precision=...]
    convert_element_type x4 -> x0, local copies, waits for them, and re-layouts: 2.56 us -> none  [the longest x2 1.71 us: shards(): point_map = (one_line[None, :, :, None] * eye[:, None, None, :]).reshape(...]
    reshape x1 -> x0, local copies, waits for them, and re-layouts: 1.33 us -> none  [shards(): source_cols.reshape(-1, 1)]
where the time goes in v2:
time: 95.7 us; the launch traced here: 95.2 us
  Pallas kernels  76.5 us (80%)
  local copies, waits for them, and re-layouts  18.1 us (19%)
    pallas_call x1, Pallas kernels, shards(): pl.pallas_call(functools.partial(kernel, row_count, col_count, kept), out...  76.5 us
    unnamed x4, local copies, waits for them, and re-layouts  18.1 us

profile of v2, /device:TPU:1, one launch (start us, length us, event | category | flops | bytes accessed | tf_op | source)
XLA Modules:
  0.0 95.2 jit_solution(10708949013479499559)
XLA Ops:
  0.6 1.4 %copy.19.project_weight = bf16[64,2]{1,0:T(8,128)(2,1)} copy(bf16[64,2]{0,1:T(2,128)(2,1)} %param.27) | data formatting | bytes 512 | tf_op args[11]
  2.0 13.0 %copy.18.spectral_weight = bf16[2,256,64,64]{3,2,1,0:T(8,128)(2,1)} copy(bf16[2,256,64,64]{1,3,2,0:T(8,128)(2,1)} %param.24) | data formatting | bytes 8388608 | tf_op args[8]
  15.0 76.5 %krylov.1 = (f32[2,64,1024]{2,1,0:T(8,128)}, f32[2,64,1024]{2,1,0:T(8,128)}) custom-call(f32[2,64,1024]{2,1,0:T(8,128)} %forcing.1, s32[64,1024]{1,0:T(8,128)} %medium.1, s32[64,1024]{1,0:T(8,128)} %mask.1, s32[16]{0:T(128)} %source_rows.1, s32[16]{0:T(128)} %source_cols.1, f32[8]{0:T(128)} %refraction.1, f32[4,64]{1,0:T(4,128)} %lift_weight.1, ...), custom_call_target="tpu_custom_call" | custom-call | tf_op jit(solution)/shard_map/krylov/pallas_call | solution.py:747
  91.4 1.9 %copy.22 = f32[2,64,1024]{2,1,0:T(8,128)} copy(f32[2,64,1024]{2,1,0:T(8,128)} %get-tuple-element.4) | data formatting | bytes 1048576
  93.3 1.9 %copy.23 = f32[2,64,1024]{2,1,0:T(8,128)} copy(f32[2,64,1024]{2,1,0:T(8,128)} %get-tuple-element.5) | data formatting | bytes 1048576

commit v3 on v2

--- a/solution.py
+++ b/solution.py
@@ -97,6 +97,8 @@
     source_rows,
     source_cols,
     refraction,
+    lift_scalars,
+    bias_scalars,
     lift_weight,
     lift_bias,
     spectral_weight,
@@ -113,7 +115,6 @@
     fwd_low,
     phase,
     weights,
-    by_mode,
     mode_map,
     project_map,
     wave_ref,
@@ -349,7 +350,7 @@
         0.0,
     )
     across = lax.dot_general(
-        project_weight[...].astype(F32), tiles, over_rows, preferred_element_type=F32
+        project_weight[...].astype(F32), tiles, (((1,), (0,)), ((), ())), preferred_element_type=F32
     )
     own_line = (
         lax.broadcasted_iota(jnp.int32, (LINES, all_rows), 0)
@@ -360,35 +361,30 @@
             own_line, across[p : p + 1, :], 0.0
         ).astype(BF16)
 
-    own_mode = (
-        lax.broadcasted_iota(jnp.int32, (8, 8 * channels), 0)
-        == lax.broadcasted_iota(jnp.int32, (8, 8 * channels), 1) // channels
-    )
-    stacked = []
-    for part in lift_parts[:2]:
-        along = jnp.concatenate([part.astype(F32)] * 8, axis=1)
-        stacked += [jnp.where(own_mode, along[g : g + 1, :], 0.0) for g in range(5)]
-    stacked = jnp.concatenate(stacked, axis=0).astype(BF16)
+    mode_of = lax.broadcasted_iota(jnp.int32, (1, 128), 1)
     weight_copy.wait()
-
-    def eight_modes(block, carry):
-        first = pl.multiple_of(8 * block, 8)
-        for part in range(2):
-            some = weights[part, pl.ds(first, 8)].reshape(8 * channels, channels)
-            both = jnp.dot(stacked, some, preferred_element_type=F32)
-            both = both[:40] + both[40:]
-            for g in range(5):
-                by_mode[part, g, pl.ds(first, 8), 0:channels] = both[8 * g : 8 * g + 8]
-        return carry
-
-    lax.fori_loop(0, kept // 8, eight_modes, 0)
-    mode_of = lax.broadcasted_iota(jnp.int32, (1, kept), 1)
-    twice = jnp.where(mode_of == 0, 1.0, 2.0)
-    anchor = jnp.where(mode_of == 0, math.sqrt(columns * row_count), 0.0)
     for part in range(2):
-        for g in range(5):
-            turned = jnp.transpose(by_mode[part, g])[:channels]
-            mode_map[part, g] = turned * (twice if g < 4 else anchor)
+        for ob in range(channels // 16):
+            outs = pl.ds(16 * ob, 16)
+            for kc in range(kept // 128):
+                some = pl.ds(128 * kc, 128)
+                used = 5 if kc == 0 else 4
+
+                def one_channel(c, sums):
+                    weight = weights[part, c, outs, some].astype(F32)
+                    factors = [lift_scalars[g, c] for g in range(4)] + [bias_scalars[c]]
+                    return tuple(x + f * weight for x, f in zip(sums, factors))
+
+                sums = lax.fori_loop(
+                    0, channels, one_channel, (jnp.zeros((16, 128), F32),) * used, unroll=8
+                )
+                twice = jnp.where(mode_of == 0, 1.0, 2.0) if kc == 0 else 2.0
+                for g in range(4):
+                    mode_map[part, g, outs, some] = sums[g] * twice
+                anchor = jnp.where(mode_of == 0, math.sqrt(columns * row_count), 0.0)
+                mode_map[part, 4, outs, some] = (
+                    sums[4] * anchor if kc == 0 else jnp.zeros((16, 128), F32)
+                )
 
     def reduced(got, source):
         got[row] = source[row]
@@ -712,6 +708,25 @@
     arrived(col_scal.at[2], 9, col_count, send_sems)
 
 
+def deliver(solution_in, residual_in, solution_out, residual_out, held, sems):
+    moves = []
+    for i, (source, target) in enumerate(
+        [(solution_in, solution_out), (residual_in, residual_out)]
+    ):
+        for p in range(2):
+            k = 2 * i + p
+            arrive = pltpu.make_async_copy(source.at[p], held.at[k], sems.at[0, k])
+            leave = pltpu.make_async_copy(held.at[k], target.at[p], sems.at[1, k])
+            moves.append((arrive, leave))
+    for arrive, _ in moves:
+        arrive.start()
+    for arrive, leave in moves:
+        arrive.wait()
+        leave.start()
+    for _, leave in moves:
+        leave.wait()
+
+
 def shards(
     row_count,
     col_count,
@@ -744,17 +759,16 @@
     smem = pl.BlockSpec(memory_space=pltpu.SMEM)
     hbm = pl.BlockSpec(memory_space=pl.ANY)
     dma = pltpu.SemaphoreType.DMA
-    return pl.pallas_call(
+    results = pl.pallas_call(
         functools.partial(kernel, row_count, col_count, kept),
         out_shape=(field, field),
-        in_specs=[vmem] * 3 + [smem] * 3 + [vmem] * 2 + [hbm] + [vmem] * 3 + [hbm] * 4,
+        in_specs=[vmem] * 3 + [smem] * 5 + [vmem] * 2 + [hbm] + [vmem] * 3 + [hbm] * 4,
         out_specs=(vmem, vmem),
         scratch_shapes=[
             pltpu.VMEM((columns, double), BF16),
             pltpu.VMEM((columns, double), BF16),
             pltpu.VMEM((8, double), F32),
-            pltpu.VMEM((2, kept, channels, channels), BF16),
-            pltpu.VMEM((2, 5, kept, 128), F32),
+            pltpu.VMEM((2, channels, channels, kept), BF16),
             pltpu.VMEM((2, 5, channels, kept), F32),
             pltpu.VMEM((2 * LINES, LINES * channels), BF16),
             pltpu.VMEM((lines, columns), F32),
@@ -796,16 +810,26 @@
         source_cols,
         refraction,
         lift_weight,
+        lift_bias,
+        lift_weight,
         lift_bias.reshape(1, -1),
-        spectral_weight,
+        spectral_weight.transpose(0, 2, 3, 1),
         point_weight,
         layer_bias.reshape(1, -1),
-        project_weight,
+        project_weight.T,
         table_high,
         table_low,
         table_back,
         phases,
     )
+    return pl.pallas_call(
+        deliver,
+        out_shape=(field, field),
+        in_specs=[hbm] * 2,
+        out_specs=[hbm] * 2,
+        scratch_shapes=[pltpu.VMEM((4, lines, columns), F32), dma((2, 4))],
+        name="deliver",
+    )(*results)
 
 
 def solution(mesh):

time: 95.7 us -> 77.5 us (0.81)
  local copies, waits for them, and re-layouts: 18.1 us -> 0 us
    unnamed x4 -> x0, local copies, waits for them, and re-layouts: 18.1 us -> none
    pallas_call x0 -> x1, Pallas kernels: none -> 1.98 us  [shards(): pl.pallas_call(deliver, out_shape=(field, field), in_specs=[hbm] * 2, out...]
    pallas_call x1, Pallas kernels: 76.5 us -> 74.6 us  [shards(): pl.pallas_call(functools.partial(kernel, row_count, col_count, kept), out...]
where the time goes in v3:
time: 77.5 us; the launch traced here: 77.3 us
  Pallas kernels  76.5 us (99%)
  between operations  0.8 us (1%)
    pallas_call x1, Pallas kernels, shards(): pl.pallas_call(functools.partial(kernel, row_count, col_count, kept), out...  74.6 us
    pallas_call x1, Pallas kernels, shards(): pl.pallas_call(deliver, out_shape=(field, field), in_specs=[hbm] * 2, out...  1.98 us

profile of v3, /device:TPU:1, one launch (start us, length us, event | category | flops | bytes accessed | tf_op | source)
XLA Modules:
  0.0 77.3 jit_solution(16737758719927629807)
XLA Ops:
  0.6 74.6 %krylov.1 = (f32[2,64,1024]{2,1,0:T(8,128)}, f32[2,64,1024]{2,1,0:T(8,128)}) custom-call(f32[2,64,1024]{2,1,0:T(8,128)} %forcing.1, s32[64,1024]{1,0:T(8,128)} %medium.1, s32[64,1024]{1,0:T(8,128)} %mask.1, s32[16]{0:T(128)} %source_rows.1, s32[16]{0:T(128)} %source_cols.1, f32[8]{0:T(128)} %refraction.1, f32[4,64]{1,0:T(4,128)} %lift_weight.1, ...), custom_call_target="tpu_custom_call" | custom-call | tf_op jit(solution)/shard_map/krylov/pallas_call | solution.py:762
  75.2 2.0 %deliver.1 = (f32[2,64,1024]{2,1,0:T(8,128)}, f32[2,64,1024]{2,1,0:T(8,128)}) custom-call(f32[2,64,1024]{2,1,0:T(8,128)} %get-tuple-element.4.solution_in, f32[2,64,1024]{2,1,0:T(8,128)} %get-tuple-element.5.residual_in), custom_call_target="tpu_custom_call" | custom-call | tf_op jit(solution)/shard_map/deliver/pallas_call | solution.py:825

commit v4 on v3

--- a/solution.py
+++ b/solution.py
@@ -24,7 +24,7 @@
 PIECE = 256
 
 
-def base_tables(tile_cols, kept_modes, grid_cols):
+def forward_tables(tile_cols, kept_modes, grid_cols):
     positions = np.arange(tile_cols, dtype=np.int64)
     mode_index = np.arange(kept_modes, dtype=np.int64)
     angles = (positions[:, None] * mode_index[None, :] % grid_cols) * (2.0 * math.pi / grid_cols)
@@ -32,15 +32,28 @@
     table = np.concatenate([np.cos(angles), -np.sin(angles)], axis=1) * scale
     high = table.astype(np.float32).astype(ml_dtypes.bfloat16)
     low = (table - high.astype(np.float64)).astype(np.float32).astype(ml_dtypes.bfloat16)
-    return high, low, np.ascontiguousarray(high.T)
-
-
-def phase_table(row_count, kept_modes):
-    tile = np.arange(row_count, dtype=np.int64)
+    return high, low
+
+
+def back_tables(tile_cols, kept_modes, grid_cols):
+    odd = 2 * np.arange(tile_cols // 2, dtype=np.int64) + 1
     mode_index = np.arange(kept_modes, dtype=np.int64)
-    angles = (tile[:, None] * mode_index[None, :] % row_count) * (2.0 * math.pi / row_count)
-    table = np.concatenate([np.cos(angles), np.sin(angles)], axis=1).astype(np.float32)
-    return np.ascontiguousarray(np.broadcast_to(table[:, None, :], (row_count, 8, 2 * kept_modes)))
+    angles = (mode_index[:, None] * odd[None, :] % (2 * grid_cols)) * (math.pi / grid_cols)
+    scale = 1.0 / math.sqrt(grid_cols)
+    table = np.stack([np.cos(angles), -np.sin(angles)]) * scale
+    return table.astype(np.float32).astype(ml_dtypes.bfloat16)
+
+
+def phase_table(row_count, tile_cols, kept_modes):
+    grid_cols = row_count * tile_cols
+    first = 2 * tile_cols * np.arange(row_count, dtype=np.int64)
+    mode_index = np.arange(kept_modes, dtype=np.int64)
+    parts = []
+    for place in (first, first + tile_cols - 1):
+        angles = (place[:, None] * mode_index[None, :] % (2 * grid_cols)) * (math.pi / grid_cols)
+        parts += [np.cos(angles), np.sin(angles)]
+    table = np.concatenate(parts, axis=1).astype(np.float32)
+    return np.ascontiguousarray(np.broadcast_to(table[:, None, :], (row_count, 8, 4 * kept_modes)))
 
 
 def split(x):
@@ -120,7 +133,8 @@
     wave_ref,
     damp_ref,
     right_ref,
-    rhs_cols,
+    even_cols,
+    odd_cols,
     mixed,
     fixed,
     modes,
@@ -148,6 +162,8 @@
     channels = point_weight.shape[0]
     groups = lines // LINES
     double = 2 * kept
+    wide = SLABS * LINES
+    half = columns // 2
     row = lax.axis_index("row")
     col = lax.axis_index("col")
     grid_scale = math.sqrt(lines * col_count * columns * row_count)
@@ -158,10 +174,14 @@
         pltpu.make_async_copy(phases.at[row], phase, table_sems.at[2]),
     ]
     back_copies = [
-        pltpu.make_async_copy(table_back, rhs_cols.at[g, pl.ds(0, double)], table_sems.at[3 + g])
+        copy
         for g in range(groups)
+        for copy in (
+            pltpu.make_async_copy(table_back.at[0], even_cols.at[g, pl.ds(0, kept)], table_sems.at[4 + 2 * g]),
+            pltpu.make_async_copy(table_back.at[1], odd_cols.at[g, pl.ds(wide, kept)], table_sems.at[5 + 2 * g]),
+        )
     ]
-    weight_copy = pltpu.make_async_copy(spectral_weight, weights, table_sems.at[3 + groups])
+    weight_copy = pltpu.make_async_copy(spectral_weight, weights, table_sems.at[3])
     for copy in [*table_copies, weight_copy, *back_copies]:
         copy.start()
 
@@ -212,25 +232,44 @@
             + jnp.dot(high[...], fwd_low[...], preferred_element_type=F32)
             + jnp.dot(low[...], fwd_high[...], preferred_element_type=F32)
         )
-        cosine, sine = phase[0:1, :kept], phase[0:1, kept:]
+        cosine, sine = phase[0:1, :kept], phase[0:1, kept:double]
         re, im = spectrum[:, :kept], spectrum[:, kept:]
         out[:, :, 0:kept] = (re * cosine + im * sine).reshape(row_count, 8, kept)
         out[:, :, kept:double] = (im * cosine - re * sine).reshape(row_count, 8, kept)
 
     def unrotated(both):
-        cosine, sine = phase[0:1, :kept], phase[0:1, kept:]
+        cosine, sine = phase[0:1, double : double + kept], phase[0:1, double + kept :]
         re, im = both[:, :kept], both[:, kept:]
         return re * cosine - im * sine, im * cosine + re * sine
 
-    def slab(g, j, value):
-        rhs_cols[g, double + LINES * j : double + LINES * (j + 1), :] = value
+    flip = jnp.where(
+        lax.broadcasted_iota(jnp.int32, (128, 128), 0)
+        + lax.broadcasted_iota(jnp.int32, (128, 128), 1)
+        == 127,
+        1.0,
+        0.0,
+    ).astype(BF16)
+
+    def reversed_lanes(x):
+        height, blocks = x.shape[0], x.shape[1] // 128
+        parts = [
+            part[:, 128 * i : 128 * i + 128] for part in three_way(x) for i in reversed(range(blocks))
+        ]
+        turned = jnp.dot(jnp.concatenate(parts, axis=0), flip, preferred_element_type=F32)
+        pieces = turned.reshape(3, blocks, height, 128)
+        total = pieces[0] + pieces[1] + pieces[2]
+        return jnp.concatenate([total[i] for i in range(blocks)], axis=1)
+
+    def slab(g, j, even, odd):
+        even_cols[g, kept + LINES * j : kept + LINES * (j + 1), :] = even
+        odd_cols[g, LINES * j : LINES * (j + 1), :] = odd
 
     def field_slabs(g, j, value):
-        top, rest = split(value)
-        slab(g, j, top)
-        slab(g, j + 1, rest)
-        slab(g, j + 2, top)
-        return top, rest
+        right, left = value[:, half:], reversed_lanes(value[:, :half])
+        even, odd = split(0.5 * (right + left)), split(0.5 * (right - left))
+        slab(g, j, even[0], odd[0])
+        slab(g, j + 1, even[1], odd[1])
+        slab(g, j + 2, even[0], odd[0])
 
     def rows_of(g):
         return slice(LINES * g, LINES * (g + 1))
@@ -259,17 +298,20 @@
         damp_ref[lines_of, :] = damping
         scaled = wave_base * refractive
         wave_ref[lines_of, :] = scaled * scaled
-        top, rest = field_slabs(g, 6, refractive)
+        field_slabs(g, 6, refractive)
+        top, rest = split(refractive)
         high[lines_of, :] = top
         low[lines_of, :] = rest
-        top, rest = field_slabs(g, 9, damping)
+        field_slabs(g, 9, damping)
+        top, rest = split(damping)
         high[lines + LINES * g : lines + LINES * (g + 1), :] = top
         low[lines + LINES * g : lines + LINES * (g + 1), :] = rest
-        ones = jnp.ones((LINES, columns), BF16)
-        slab(g, 12, ones)
-        slab(g, 13, ones)
-        slab(g, 14, jnp.zeros_like(ones))
-        slab(g, 15, jnp.zeros_like(ones))
+        ones = jnp.ones((LINES, half), BF16)
+        zeros = jnp.zeros_like(ones)
+        slab(g, 12, ones, zeros)
+        slab(g, 13, ones, zeros)
+        slab(g, 14, zeros, zeros)
+        slab(g, 15, zeros, zeros)
     for copy in table_copies:
         copy.wait()
     forward(send_feat)
@@ -325,7 +367,6 @@
     channel_row = lax.broadcasted_iota(jnp.int32, (8, channels), 0)
     point = point + jnp.where(channel_row == 4, layer_bias[...], 0.0)
     top, rest = split(point)
-    wide = SLABS * LINES
     from_row = lax.broadcasted_iota(jnp.int32, (8, wide), 0)
     slab_of = lax.broadcasted_iota(jnp.int32, (8, wide), 1) // LINES
     first_slab = 3 * from_row
@@ -341,7 +382,7 @@
     for i in range(LINES):
         masked = jnp.where(line_of == i, spread_out, 0.0).astype(BF16)
         for g in range(groups):
-            mixed[LINES * g + i, :, double:] = masked
+            mixed[LINES * g + i, :, kept : kept + wide] = masked
     all_rows = LINES * channels
     tiles = jnp.where(
         lax.broadcasted_iota(jnp.int32, (channels, all_rows), 0)
@@ -419,6 +460,7 @@
 
     def mix_lines(first, count, kc, ob, channels_in, bias, source, store):
         low_k, high_k = pl.ds(128 * kc, 128), pl.ds(kept + 128 * kc, 128)
+        store_k = pl.ds(store.shape[2] - kept + 128 * kc, 128)
         outs = pl.ds(16 * ob, 16)
         maps = [(mode_map[0, g, outs, low_k], mode_map[1, g, outs, low_k]) for g in channels_in]
         start = (mode_map[0, 4, outs, low_k], mode_map[1, 4, outs, low_k]) if bias else None
@@ -438,7 +480,7 @@
                     re = re + (map_re * one_re - map_im * one_im)
                     im = im + (map_re * one_im + map_im * one_re)
                 store[line, outs, low_k] = re.astype(store.dtype)
-                store[line, outs, high_k] = im.astype(store.dtype)
+                store[line, outs, store_k] = im.astype(store.dtype)
 
     def mix_fixed():
         for kc in range(kept // 128):
@@ -457,33 +499,44 @@
                 mix_lines(LINES * g, LINES, kc, ob, (0, 1), False, fixed, mixed)
 
     def layer(step):
-        last = columns // PIECE - 1
-        edges = [(g, n) for g in range(groups) for n in sorted({0, last})]
-        ends = [(g, n) for g in sorted({0, groups - 1}) for n in range(1, last)]
-        inside = [(g, n) for g in range(1, groups - 1) for n in range(1, last)]
+        outer = half // PIECE - 1
+        edges = [(g, outer) for g in range(groups)]
+        ends = [(g, n) for g in sorted({0, groups - 1}) for n in range(outer)]
+        inside = [(g, n) for g in range(1, groups - 1) for n in range(outer)]
         order = edges + ends + inside
         copies = halo_copies(step)
 
         def multiply(g, n, slot):
-            left = mixed[LINES * g : LINES * (g + 1)].reshape(LINES * channels, double + SLABS * LINES)
-            before[slot] = jnp.dot(
-                left, rhs_cols[g, :, PIECE * n : PIECE * (n + 1)], preferred_element_type=F32
+            left = mixed[LINES * g : LINES * (g + 1)].reshape(LINES * channels, double + wide)
+            piece = slice(PIECE * n, PIECE * (n + 1))
+            before[slot, 0] = jnp.dot(
+                left[:, : kept + wide], even_cols[g, :, piece], preferred_element_type=F32
             )
+            before[slot, 1] = jnp.dot(
+                left[:, kept:], odd_cols[g, :, piece], preferred_element_type=F32
+            )
 
         def finish(g, n, slot):
-            active = gelu(before[slot]).astype(BF16)
-            out = jnp.dot(project_map[...], active, preferred_element_type=F32)
-            first = 8 + LINES * g
-            place = slice(128 + PIECE * n, 128 + PIECE * (n + 1))
-            ext[step, 0, first : first + LINES, place] = out[:LINES]
-            ext[step, 1, first : first + LINES, place] = out[LINES:]
+            lines_of = slice(8 + LINES * g, 8 + LINES * (g + 1))
+            even, odd = before[slot, 0], before[slot, 1]
+            for side in range(2):
+                active = gelu(even + odd if side else even - odd).astype(BF16)
+                out = jnp.dot(project_map[...], active, preferred_element_type=F32)
+                if side:
+                    first = 128 + half + PIECE * n
+                else:
+                    first = 128 + half - PIECE * (n + 1)
+                    out = reversed_lanes(out)
+                place = slice(first, first + PIECE)
+                ext[step, 0, lines_of, place] = out[:LINES]
+                ext[step, 1, lines_of, place] = out[LINES:]
 
         mix_group(0)
         for t in range(len(order) + 1):
             if t < len(order):
                 g, n = order[t]
                 multiply(g, n, t % 2)
-                if t < len(edges) and n == 0 and g + 1 < groups:
+                if t < len(edges) and g + 1 < groups:
                     mix_group(g + 1)
             if t > 0:
                 finish(*order[t - 1], (t - 1) % 2)
@@ -751,8 +804,9 @@
     double = 2 * kept
     assert row_count * 8 == 2 * lines
 
-    table_high, table_low, table_back = base_tables(columns, kept, grid_cols)
-    phases = phase_table(row_count, kept)
+    table_high, table_low = forward_tables(columns, kept, grid_cols)
+    table_back = back_tables(columns, kept, grid_cols)
+    phases = phase_table(row_count, columns, kept)
 
     field = jax.ShapeDtypeStruct((2, lines, columns), F32)
     vmem = pl.BlockSpec(memory_space=pltpu.VMEM)
@@ -767,14 +821,15 @@
         scratch_shapes=[
             pltpu.VMEM((columns, double), BF16),
             pltpu.VMEM((columns, double), BF16),
-            pltpu.VMEM((8, double), F32),
+            pltpu.VMEM((8, 2 * double), F32),
             pltpu.VMEM((2, channels, channels, kept), BF16),
             pltpu.VMEM((2, 5, channels, kept), F32),
             pltpu.VMEM((2 * LINES, LINES * channels), BF16),
             pltpu.VMEM((lines, columns), F32),
             pltpu.VMEM((lines, columns), F32),
             pltpu.VMEM((2, lines, columns), F32),
-            pltpu.VMEM((groups, double + SLABS * LINES, columns), BF16),
+            pltpu.VMEM((groups, kept + SLABS * LINES, columns // 2), BF16),
+            pltpu.VMEM((groups, kept + SLABS * LINES, columns // 2), BF16),
             pltpu.VMEM((lines, channels, double + SLABS * LINES), BF16),
             pltpu.VMEM((lines, channels, double), F32),
             pltpu.VMEM((4, lines, double), F32),
@@ -788,11 +843,11 @@
             pltpu.VMEM((2, row_count, 8, double), F32),
             pltpu.VMEM((row_count, 8, 128), F32),
             pltpu.VMEM((3, col_count, 8, 128), F32),
-            pltpu.VMEM((2, LINES * channels, PIECE), F32),
+            pltpu.VMEM((2, 2, LINES * channels, PIECE), F32),
             pltpu.VMEM((2, 2, lines + 16, columns + 256), F32),
             pltpu.VMEM((2, 2, lines, columns), F32),
             pltpu.VMEM((2, lines, columns), F32),
-            dma((4 + groups,)),
+            dma((4 + 2 * groups,)),
             dma((2, 8)),
             dma((2, 8)),
             dma((10,)),

time: 77.5 us -> 76.6 us (0.988)
  Pallas kernels: 76.5 us -> 75.7 us
    pallas_call x1, Pallas kernels: 74.6 us -> 73.7 us  [shards(): pl.pallas_call(functools.partial(kernel, row_count, col_count, kept), out...]
where the time goes in v4:
time: 76.6 us; the launch traced here: 76.5 us
  Pallas kernels  75.7 us (99%)
  between operations  0.8 us (1%)
    pallas_call x1, Pallas kernels, shards(): pl.pallas_call(functools.partial(kernel, row_count, col_count, kept), out...  73.7 us
    pallas_call x1, Pallas kernels, shards(): pl.pallas_call(deliver, out_shape=(field, field), in_specs=[hbm] * 2, out...  1.98 us

profile of v4, /device:TPU:1, one launch (start us, length us, event | category | flops | bytes accessed | tf_op | source)
XLA Modules:
  0.0 76.5 jit_solution(4672146533293118129)
XLA Ops:
  0.6 73.7 %krylov.1 = (f32[2,64,1024]{2,1,0:T(8,128)}, f32[2,64,1024]{2,1,0:T(8,128)}) custom-call(f32[2,64,1024]{2,1,0:T(8,128)} %forcing.1, s32[64,1024]{1,0:T(8,128)} %medium.1, s32[64,1024]{1,0:T(8,128)} %mask.1, s32[16]{0:T(128)} %source_rows.1, s32[16]{0:T(128)} %source_cols.1, f32[8]{0:T(128)} %refraction.1, f32[4,64]{1,0:T(4,128)} %lift_weight.1, ...), custom_call_target="tpu_custom_call" | custom-call | tf_op jit(solution)/shard_map/krylov/pallas_call | solution.py:816
  74.3 2.0 %deliver.1 = (f32[2,64,1024]{2,1,0:T(8,128)}, f32[2,64,1024]{2,1,0:T(8,128)}) custom-call(f32[2,64,1024]{2,1,0:T(8,128)} %get-tuple-element.4.solution_in, f32[2,64,1024]{2,1,0:T(8,128)} %get-tuple-element.5.residual_in), custom_call_target="tpu_custom_call" | custom-call | tf_op jit(solution)/shard_map/deliver/pallas_call | solution.py:880

commit v5 on v4

--- a/solution.py
+++ b/solution.py
@@ -131,7 +131,7 @@
     mode_map,
     project_map,
     wave_ref,
-    damp_ref,
+    feature_ref,
     right_ref,
     even_cols,
     odd_cols,
@@ -226,11 +226,11 @@
         whole = target.at[pl.ds(0, count - 1)]
         pltpu.make_async_copy(whole, whole, sems.at[index]).wait()
 
-    def forward(out):
+    def forward(kind, out):
         spectrum = (
-            jnp.dot(high[...], fwd_high[...], preferred_element_type=F32)
-            + jnp.dot(high[...], fwd_low[...], preferred_element_type=F32)
-            + jnp.dot(low[...], fwd_high[...], preferred_element_type=F32)
+            jnp.dot(high[kind], fwd_high[...], preferred_element_type=F32)
+            + jnp.dot(high[kind], fwd_low[...], preferred_element_type=F32)
+            + jnp.dot(low[kind], fwd_high[...], preferred_element_type=F32)
         )
         cosine, sine = phase[0:1, :kept], phase[0:1, kept:double]
         re, im = spectrum[:, :kept], spectrum[:, kept:]
@@ -295,26 +295,18 @@
         for level in range(refraction.shape[0]):
             refractive = jnp.where(kind == level, refraction[level], refractive)
         damping = 0.1 + mask[lines_of, :].astype(F32)
-        damp_ref[lines_of, :] = damping
         scaled = wave_base * refractive
         wave_ref[lines_of, :] = scaled * scaled
-        field_slabs(g, 6, refractive)
-        top, rest = split(refractive)
-        high[lines_of, :] = top
-        low[lines_of, :] = rest
-        field_slabs(g, 9, damping)
-        top, rest = split(damping)
-        high[lines + LINES * g : lines + LINES * (g + 1), :] = top
-        low[lines + LINES * g : lines + LINES * (g + 1), :] = rest
-        ones = jnp.ones((LINES, half), BF16)
-        zeros = jnp.zeros_like(ones)
-        slab(g, 12, ones, zeros)
-        slab(g, 13, ones, zeros)
-        slab(g, 14, zeros, zeros)
-        slab(g, 15, zeros, zeros)
+        feature_ref[0, lines_of, :] = refractive
+        feature_ref[1, lines_of, :] = damping
+        for i, feature in enumerate((refractive, damping)):
+            top, rest = split(feature)
+            place = slice(lines * i + LINES * g, lines * i + LINES * (g + 1))
+            high[0, place, :] = top
+            low[0, place, :] = rest
     for copy in table_copies:
         copy.wait()
-    forward(send_feat)
+    forward(0, send_feat)
     pl.semaphore_wait(barrier, greeted)
     spread(lambda there: send_feat.at[there], got_feat, 0, "row", row, row_count)
 
@@ -345,10 +337,10 @@
             right_ref[p, lines_of, :] = field
             square = square + folded(field * field)
             top, rest = split(field)
-            high[p * lines + LINES * g : p * lines + LINES * (g + 1), :] = top
-            low[p * lines + LINES * g : p * lines + LINES * (g + 1), :] = rest
+            high[1, p * lines + LINES * g : p * lines + LINES * (g + 1), :] = top
+            low[1, p * lines + LINES * g : p * lines + LINES * (g + 1), :] = rest
     def send_modes(step, tile):
-        forward(send_wave.at[step])
+        forward(1, send_wave.at[step])
         for r in range(row_count):
             send_wave[step, r, :, double:] = tile
         spread(
@@ -356,6 +348,251 @@
         )
 
     send_modes(0, scalar_tile([square]))
+
+    mode_of = lax.broadcasted_iota(jnp.int32, (1, 128), 1)
+
+    def fold(ob, kc):
+        outs, some = pl.ds(16 * ob, 16), pl.ds(128 * kc, 128)
+        used = 5 if kc == 0 else 4
+        twice = jnp.where(mode_of == 0, 1.0, 2.0) if kc == 0 else 2.0
+        both = []
+        for part in range(2):
+
+            def one_channel(c, sums):
+                weight = weights[part, c, outs, some].astype(F32)
+                factors = [lift_scalars[g, c] for g in range(4)] + [bias_scalars[c]]
+                return tuple(x + f * weight for x, f in zip(sums, factors))
+
+            both.append(
+                lax.fori_loop(
+                    0, channels, one_channel, (jnp.zeros((16, 128), F32),) * used, unroll=8
+                )
+            )
+        for g in range(4):
+            re, im = both[0][g] * twice, both[1][g] * twice
+            mode_map[0, g, outs, some] = re
+            mode_map[1, g, outs, some] = re + im
+            mode_map[2, g, outs, some] = im - re
+        anchor = jnp.where(mode_of == 0, math.sqrt(columns * row_count), 0.0)
+        for part in range(2):
+            mode_map[part, 4, outs, some] = (
+                both[part][4] * anchor if kc == 0 else jnp.zeros((16, 128), F32)
+            )
+
+    def reduced(got, source):
+        got[row] = source[row]
+        total = got[0]
+        for r in range(1, row_count):
+            total = total + got[r]
+        return total
+
+    blocks = [(ob, kc) for ob in range(channels // 16) for kc in range(kept // 128)]
+    weight_copy.wait()
+    for block in blocks[: len(blocks) // 2]:
+        fold(*block)
+    arrived(got_feat, 0, row_count, recv_sems)
+    all_feat[row] = reduced(got_feat, send_feat)
+    spread(lambda there: all_feat.at[row], all_feat, 1, "row", row, row_count)
+
+    def wave_reduce(step):
+        index = 2 + 3 * step
+        arrived(got_wave.at[step], index, row_count, recv_sems)
+        total = reduced(got_wave.at[step], send_wave.at[step])
+        all_wave[step, row] = total[:, :double]
+        spread(
+            lambda there: all_wave.at[step, row], all_wave.at[step], index + 1, "row", row, row_count
+        )
+        col_scal[step, col] = total[:, double:]
+        spread(
+            lambda there: col_scal.at[step, col], col_scal.at[step], index + 2, "col", col, col_count
+        )
+
+    def col_total(step):
+        arrived(col_scal.at[step], 4 + 3 * step, col_count, recv_sems)
+        total = col_scal[step, 0]
+        for r in range(1, col_count):
+            total = total + col_scal[step, r]
+        return jnp.sum(total, axis=1, keepdims=True)
+
+    def mix_lines(first, count, kc, ob, channels_in, bias, source, store):
+        low_k, high_k = pl.ds(128 * kc, 128), pl.ds(kept + 128 * kc, 128)
+        store_k = pl.ds(store.shape[2] - kept + 128 * kc, 128)
+        outs = pl.ds(16 * ob, 16)
+        maps = [tuple(mode_map[i, g, outs, low_k] for i in range(3)) for g in channels_in]
+        start = (mode_map[0, 4, outs, low_k], mode_map[1, 4, outs, low_k]) if bias else None
+        for block in range(count // 8):
+            top = first + 8 * block
+            parts = [
+                (modes[g, pl.ds(top, 8), low_k], modes[g, pl.ds(top, 8), high_k]) for g in channels_in
+            ]
+            parts = [(mode_re, mode_im, mode_re + mode_im) for mode_re, mode_im in parts]
+            for i in range(8):
+                line = top + i
+                if bias:
+                    re, im = start
+                else:
+                    re, im = source[line, outs, low_k], source[line, outs, high_k]
+                shared = None
+                for (mode_re, mode_im, mode_sum), (map_re, map_sum, map_less) in zip(parts, maps):
+                    product = map_re * mode_sum[i : i + 1]
+                    shared = product if shared is None else shared + product
+                    re = re - map_sum * mode_im[i : i + 1]
+                    im = im + map_less * mode_re[i : i + 1]
+                re, im = re + shared, im + shared
+                store[line, outs, low_k] = re.astype(store.dtype)
+                store[line, outs, store_k] = im.astype(store.dtype)
+
+    def mix_fixed():
+        for kc in range(kept // 128):
+            for ob in range(channels // 16):
+
+                def eight_lines(block, carry):
+                    first = pl.multiple_of(8 * block, 8)
+                    mix_lines(first, 8, kc, ob, (2, 3), True, None, fixed)
+                    return carry
+
+                lax.fori_loop(0, lines // 8, eight_lines, 0)
+
+    def mix_group(g):
+        for kc in range(kept // 128):
+            for ob in range(channels // 16):
+                mix_lines(LINES * g, LINES, kc, ob, (0, 1), False, fixed, mixed)
+
+    def layer(step):
+        outer = half // PIECE - 1
+        edges = [(g, outer) for g in range(groups)]
+        ends = [(g, n) for g in sorted({0, groups - 1}) for n in range(outer)]
+        inside = [(g, n) for g in range(1, groups - 1) for n in range(outer)]
+        order = edges + ends + inside
+        copies = halo_copies(step)
+
+        def multiply(g, n, slot):
+            left = mixed[LINES * g : LINES * (g + 1)].reshape(LINES * channels, double + wide)
+            piece = slice(PIECE * n, PIECE * (n + 1))
+            before[slot, 0] = jnp.dot(
+                left[:, : kept + wide], even_cols[g, :, piece], preferred_element_type=F32
+            )
+            before[slot, 1] = jnp.dot(
+                left[:, kept:], odd_cols[g, :, piece], preferred_element_type=F32
+            )
+
+        def finish(g, n, slot):
+            lines_of = slice(8 + LINES * g, 8 + LINES * (g + 1))
+            even, odd = before[slot, 0], before[slot, 1]
+            for side in range(2):
+                active = gelu(even + odd if side else even - odd).astype(BF16)
+                out = jnp.dot(project_map[...], active, preferred_element_type=F32)
+                if side:
+                    first = 128 + half + PIECE * n
+                else:
+                    first = 128 + half - PIECE * (n + 1)
+                    out = reversed_lanes(out)
+                place = slice(first, first + PIECE)
+                ext[step, 0, lines_of, place] = out[:LINES]
+                ext[step, 1, lines_of, place] = out[LINES:]
+
+        mix_group(0)
+        for t in range(len(order) + 1):
+            if t < len(order):
+                g, n = order[t]
+                multiply(g, n, t % 2)
+                if t < len(edges) and g + 1 < groups:
+                    mix_group(g + 1)
+            if t > 0:
+                finish(*order[t - 1], (t - 1) % 2)
+            if t == len(edges):
+                for i in (0, 1, 4, 5, 6, 7):
+                    copies[i].start()
+            if t == len(edges) + len(ends):
+                for i in (2, 3):
+                    copies[i].start()
+
+    def halo_copies(step):
+        tall, across_all = pl.ds(8, lines), pl.ds(128, columns)
+        line_ends = {
+            1: (pl.ds(lines, 8), pl.ds(0, 8)),
+            -1: (pl.ds(8, 8), pl.ds(8 + lines, 8)),
+            0: (tall, tall),
+        }
+        col_ends = {
+            1: (pl.ds(columns, 128), pl.ds(0, 128)),
+            -1: (pl.ds(128, 128), pl.ds(128 + columns, 128)),
+            0: (across_all, across_all),
+        }
+        copies = []
+        for i, (dr, dc) in enumerate(
+            [(1, 0), (-1, 0), (0, 1), (0, -1), (1, 1), (1, -1), (-1, 1), (-1, -1)]
+        ):
+            here_l, there_l = line_ends[dc]
+            here_c, there_c = col_ends[dr]
+            copies.append(
+                pltpu.make_async_remote_copy(
+                    src_ref=ext.at[step, :, here_l, here_c],
+                    dst_ref=ext.at[step, :, there_l, there_c],
+                    send_sem=halo_send.at[step, i],
+                    recv_sem=halo_recv.at[step, i],
+                    device_id={
+                        "row": lax.rem(row + dr + row_count, row_count),
+                        "col": lax.rem(col + dc + col_count, col_count),
+                    },
+                    device_id_type=MESH,
+                )
+            )
+        return copies
+
+    def halos(step):
+        for copy in halo_copies(step):
+            copy.wait()
+        view = ext.at[step]
+
+        @pl.when(row == 0)
+        def _():
+            view[:, :, 0:128] = jnp.zeros((2, lines + 16, 128), F32)
+
+        @pl.when(row == row_count - 1)
+        def _():
+            view[:, :, 128 + columns :] = jnp.zeros((2, lines + 16, 128), F32)
+
+        @pl.when(col == 0)
+        def _():
+            view[:, 0:8, :] = jnp.zeros((2, 8, columns + 256), F32)
+
+        @pl.when(col == col_count - 1)
+        def _():
+            view[:, 8 + lines :, :] = jnp.zeros((2, 8, columns + 256), F32)
+
+    def operate(step, g):
+        laps, fields = [], []
+        for p in range(2):
+            first = 8 + LINES * g
+            beside = (
+                ext[step, p, first - 1 : first - 1 + LINES, :]
+                + ext[step, p, first + 1 : first + 1 + LINES, :]
+            )
+            centre = ext[step, p, first : first + LINES, :]
+            both = 4.0 * centre + beside
+            width = columns + 256
+            around = pltpu.roll(both, 1, 1) + pltpu.roll(both, width - 1, 1)
+            total = (4.0 * beside - 20.0 * centre + around) * (1.0 / 6.0)
+            laps.append(total[:, 128 : 128 + columns])
+            fields.append(centre[:, 128 : 128 + columns])
+        wave, damping = wave_ref[rows_of(g), :], feature_ref[1, rows_of(g), :]
+        real = -laps[0] - wave * (fields[0] + damping * fields[1])
+        imag = -laps[1] - wave * (fields[1] - damping * fields[0])
+        return real, imag
+
+    def pair(first, second):
+        return (
+            folded(first[0] * second[0] + first[1] * second[1]),
+            folded(first[0] * second[1] - first[1] * second[0]),
+        )
+
+    def add(a, b):
+        return [x + y for x, y in zip(a, b)]
+
+    for block in blocks[len(blocks) // 2 :]:
+        fold(*block)
+    wave_reduce(0)
 
     lift = jnp.concatenate(
         [lift_weight[...], lift_bias[...], jnp.zeros((3, channels), F32)], axis=0
@@ -402,235 +639,16 @@
             own_line, across[p : p + 1, :], 0.0
         ).astype(BF16)
 
-    mode_of = lax.broadcasted_iota(jnp.int32, (1, 128), 1)
-    weight_copy.wait()
-    for part in range(2):
-        for ob in range(channels // 16):
-            outs = pl.ds(16 * ob, 16)
-            for kc in range(kept // 128):
-                some = pl.ds(128 * kc, 128)
-                used = 5 if kc == 0 else 4
-
-                def one_channel(c, sums):
-                    weight = weights[part, c, outs, some].astype(F32)
-                    factors = [lift_scalars[g, c] for g in range(4)] + [bias_scalars[c]]
-                    return tuple(x + f * weight for x, f in zip(sums, factors))
-
-                sums = lax.fori_loop(
-                    0, channels, one_channel, (jnp.zeros((16, 128), F32),) * used, unroll=8
-                )
-                twice = jnp.where(mode_of == 0, 1.0, 2.0) if kc == 0 else 2.0
-                for g in range(4):
-                    mode_map[part, g, outs, some] = sums[g] * twice
-                anchor = jnp.where(mode_of == 0, math.sqrt(columns * row_count), 0.0)
-                mode_map[part, 4, outs, some] = (
-                    sums[4] * anchor if kc == 0 else jnp.zeros((16, 128), F32)
-                )
-
-    def reduced(got, source):
-        got[row] = source[row]
-        total = got[0]
-        for r in range(1, row_count):
-            total = total + got[r]
-        return total
-
-    arrived(got_feat, 0, row_count, recv_sems)
-    all_feat[row] = reduced(got_feat, send_feat)
-    spread(lambda there: all_feat.at[row], all_feat, 1, "row", row, row_count)
-
-    def wave_reduce(step):
-        index = 2 + 3 * step
-        arrived(got_wave.at[step], index, row_count, recv_sems)
-        total = reduced(got_wave.at[step], send_wave.at[step])
-        all_wave[step, row] = total[:, :double]
-        spread(
-            lambda there: all_wave.at[step, row], all_wave.at[step], index + 1, "row", row, row_count
-        )
-        col_scal[step, col] = total[:, double:]
-        spread(
-            lambda there: col_scal.at[step, col], col_scal.at[step], index + 2, "col", col, col_count
-        )
-
-    def col_total(step):
-        arrived(col_scal.at[step], 4 + 3 * step, col_count, recv_sems)
-        total = col_scal[step, 0]
-        for r in range(1, col_count):
-            total = total + col_scal[step, r]
-        return jnp.sum(total, axis=1, keepdims=True)
-
-    def mix_lines(first, count, kc, ob, channels_in, bias, source, store):
-        low_k, high_k = pl.ds(128 * kc, 128), pl.ds(kept + 128 * kc, 128)
-        store_k = pl.ds(store.shape[2] - kept + 128 * kc, 128)
-        outs = pl.ds(16 * ob, 16)
-        maps = [(mode_map[0, g, outs, low_k], mode_map[1, g, outs, low_k]) for g in channels_in]
-        start = (mode_map[0, 4, outs, low_k], mode_map[1, 4, outs, low_k]) if bias else None
-        for block in range(count // 8):
-            top = first + 8 * block
-            parts = [
-                (modes[g, pl.ds(top, 8), low_k], modes[g, pl.ds(top, 8), high_k]) for g in channels_in
-            ]
-            for i in range(8):
-                line = top + i
-                if bias:
-                    re, im = start
-                else:
-                    re, im = source[line, outs, low_k], source[line, outs, high_k]
-                for (mode_re, mode_im), (map_re, map_im) in zip(parts, maps):
-                    one_re, one_im = mode_re[i : i + 1], mode_im[i : i + 1]
-                    re = re + (map_re * one_re - map_im * one_im)
-                    im = im + (map_re * one_im + map_im * one_re)
-                store[line, outs, low_k] = re.astype(store.dtype)
-                store[line, outs, store_k] = im.astype(store.dtype)
-
-    def mix_fixed():
-        for kc in range(kept // 128):
-            for ob in range(channels // 16):
-
-                def eight_lines(block, carry):
-                    first = pl.multiple_of(8 * block, 8)
-                    mix_lines(first, 8, kc, ob, (2, 3), True, None, fixed)
-                    return carry
-
-                lax.fori_loop(0, lines // 8, eight_lines, 0)
-
-    def mix_group(g):
-        for kc in range(kept // 128):
-            for ob in range(channels // 16):
-                mix_lines(LINES * g, LINES, kc, ob, (0, 1), False, fixed, mixed)
-
-    def layer(step):
-        outer = half // PIECE - 1
-        edges = [(g, outer) for g in range(groups)]
-        ends = [(g, n) for g in sorted({0, groups - 1}) for n in range(outer)]
-        inside = [(g, n) for g in range(1, groups - 1) for n in range(outer)]
-        order = edges + ends + inside
-        copies = halo_copies(step)
-
-        def multiply(g, n, slot):
-            left = mixed[LINES * g : LINES * (g + 1)].reshape(LINES * channels, double + wide)
-            piece = slice(PIECE * n, PIECE * (n + 1))
-            before[slot, 0] = jnp.dot(
-                left[:, : kept + wide], even_cols[g, :, piece], preferred_element_type=F32
-            )
-            before[slot, 1] = jnp.dot(
-                left[:, kept:], odd_cols[g, :, piece], preferred_element_type=F32
-            )
-
-        def finish(g, n, slot):
-            lines_of = slice(8 + LINES * g, 8 + LINES * (g + 1))
-            even, odd = before[slot, 0], before[slot, 1]
-            for side in range(2):
-                active = gelu(even + odd if side else even - odd).astype(BF16)
-                out = jnp.dot(project_map[...], active, preferred_element_type=F32)
-                if side:
-                    first = 128 + half + PIECE * n
-                else:
-                    first = 128 + half - PIECE * (n + 1)
-                    out = reversed_lanes(out)
-                place = slice(first, first + PIECE)
-                ext[step, 0, lines_of, place] = out[:LINES]
-                ext[step, 1, lines_of, place] = out[LINES:]
-
-        mix_group(0)
-        for t in range(len(order) + 1):
-            if t < len(order):
-                g, n = order[t]
-                multiply(g, n, t % 2)
-                if t < len(edges) and g + 1 < groups:
-                    mix_group(g + 1)
-            if t > 0:
-                finish(*order[t - 1], (t - 1) % 2)
-            if t == len(edges):
-                for i in (0, 1, 4, 5, 6, 7):
-                    copies[i].start()
-            if t == len(edges) + len(ends):
-                for i in (2, 3):
-                    copies[i].start()
-
-    def halo_copies(step):
-        tall, across_all = pl.ds(8, lines), pl.ds(128, columns)
-        line_ends = {
-            1: (pl.ds(lines, 8), pl.ds(0, 8)),
-            -1: (pl.ds(8, 8), pl.ds(8 + lines, 8)),
-            0: (tall, tall),
-        }
-        col_ends = {
-            1: (pl.ds(columns, 128), pl.ds(0, 128)),
-            -1: (pl.ds(128, 128), pl.ds(128 + columns, 128)),
-            0: (across_all, across_all),
-        }
-        copies = []
-        for i, (dr, dc) in enumerate(
-            [(1, 0), (-1, 0), (0, 1), (0, -1), (1, 1), (1, -1), (-1, 1), (-1, -1)]
-        ):
-            here_l, there_l = line_ends[dc]
-            here_c, there_c = col_ends[dr]
-            copies.append(
-                pltpu.make_async_remote_copy(
-                    src_ref=ext.at[step, :, here_l, here_c],
-                    dst_ref=ext.at[step, :, there_l, there_c],
-                    send_sem=halo_send.at[step, i],
-                    recv_sem=halo_recv.at[step, i],
-                    device_id={
-                        "row": lax.rem(row + dr + row_count, row_count),
-                        "col": lax.rem(col + dc + col_count, col_count),
-                    },
-                    device_id_type=MESH,
-                )
-            )
-        return copies
-
-    def halos(step):
-        for copy in halo_copies(step):
-            copy.wait()
-        view = ext.at[step]
-
-        @pl.when(row == 0)
-        def _():
-            view[:, :, 0:128] = jnp.zeros((2, lines + 16, 128), F32)
-
-        @pl.when(row == row_count - 1)
-        def _():
-            view[:, :, 128 + columns :] = jnp.zeros((2, lines + 16, 128), F32)
-
-        @pl.when(col == 0)
-        def _():
-            view[:, 0:8, :] = jnp.zeros((2, 8, columns + 256), F32)
-
-        @pl.when(col == col_count - 1)
-        def _():
-            view[:, 8 + lines :, :] = jnp.zeros((2, 8, columns + 256), F32)
-
-    def operate(step, g):
-        laps, fields = [], []
-        for p in range(2):
-            first = 8 + LINES * g
-            beside = (
-                ext[step, p, first - 1 : first - 1 + LINES, :]
-                + ext[step, p, first + 1 : first + 1 + LINES, :]
-            )
-            centre = ext[step, p, first : first + LINES, :]
-            both = 4.0 * centre + beside
-            width = columns + 256
-            around = pltpu.roll(both, 1, 1) + pltpu.roll(both, width - 1, 1)
-            total = (4.0 * beside - 20.0 * centre + around) * (1.0 / 6.0)
-            laps.append(total[:, 128 : 128 + columns])
-            fields.append(centre[:, 128 : 128 + columns])
-        wave, damping = wave_ref[rows_of(g), :], damp_ref[rows_of(g), :]
-        real = -laps[0] - wave * (fields[0] + damping * fields[1])
-        imag = -laps[1] - wave * (fields[1] - damping * fields[0])
-        return real, imag
-
-    def pair(first, second):
-        return (
-            folded(first[0] * second[0] + first[1] * second[1]),
-            folded(first[0] * second[1] - first[1] * second[0]),
-        )
-
-    def add(a, b):
-        return [x + y for x, y in zip(a, b)]
-
-    wave_reduce(0)
+    for g in range(groups):
+        ones = jnp.ones((LINES, half), BF16)
+        zeros = jnp.zeros_like(ones)
+        slab(g, 12, ones, zeros)
+        slab(g, 13, ones, zeros)
+        slab(g, 14, zeros, zeros)
+        slab(g, 15, zeros, zeros)
+        for i in range(2):
+            field_slabs(g, 6 + 3 * i, feature_ref[i, rows_of(g), :])
+
     arrived(all_feat, 1, row_count, recv_sems)
     re, im = unrotated(all_feat[...].reshape(2 * lines, double))
     for g in range(2):
@@ -660,8 +678,8 @@
         for p in range(2):
             applied[0, p, lines_of, :] = result[p]
             top, rest = split(result[p])
-            high[p * lines + LINES * g : p * lines + LINES * (g + 1), :] = top
-            low[p * lines + LINES * g : p * lines + LINES * (g + 1), :] = rest
+            high[1, p * lines + LINES * g : p * lines + LINES * (g + 1), :] = top
+            low[1, p * lines + LINES * g : p * lines + LINES * (g + 1), :] = rest
         start = (right_ref[0, lines_of, :], right_ref[1, lines_of, :])
         square = folded(result[0] * result[0] + result[1] * result[1])
         sums = add(sums, (*pair(start, result), square))
@@ -761,23 +779,15 @@
     arrived(col_scal.at[2], 9, col_count, send_sems)
 
 
-def deliver(solution_in, residual_in, solution_out, residual_out, held, sems):
-    moves = []
-    for i, (source, target) in enumerate(
-        [(solution_in, solution_out), (residual_in, residual_out)]
-    ):
-        for p in range(2):
-            k = 2 * i + p
-            arrive = pltpu.make_async_copy(source.at[p], held.at[k], sems.at[0, k])
-            leave = pltpu.make_async_copy(held.at[k], target.at[p], sems.at[1, k])
-            moves.append((arrive, leave))
-    for arrive, _ in moves:
-        arrive.start()
-    for arrive, leave in moves:
-        arrive.wait()
-        leave.start()
-    for _, leave in moves:
-        leave.wait()
+def deliver(solution_in, residual_in, solution_out, residual_out, sems):
+    copies = [
+        pltpu.make_async_copy(solution_in, solution_out, sems.at[0]),
+        pltpu.make_async_copy(residual_in, residual_out, sems.at[1]),
+    ]
+    for copy in copies:
+        copy.start()
+    for copy in copies:
+        copy.wait()
 
 
 def shards(
@@ -815,7 +825,7 @@
     dma = pltpu.SemaphoreType.DMA
     results = pl.pallas_call(
         functools.partial(kernel, row_count, col_count, kept),
-        out_shape=(field, field),
+        out_shape=(pltpu.VMEM(field.shape, F32), pltpu.VMEM(field.shape, F32)),
         in_specs=[vmem] * 3 + [smem] * 5 + [vmem] * 2 + [hbm] + [vmem] * 3 + [hbm] * 4,
         out_specs=(vmem, vmem),
         scratch_shapes=[
@@ -823,18 +833,18 @@
             pltpu.VMEM((columns, double), BF16),
             pltpu.VMEM((8, 2 * double), F32),
             pltpu.VMEM((2, channels, channels, kept), BF16),
-            pltpu.VMEM((2, 5, channels, kept), F32),
+            pltpu.VMEM((3, 5, channels, kept), F32),
             pltpu.VMEM((2 * LINES, LINES * channels), BF16),
             pltpu.VMEM((lines, columns), F32),
-            pltpu.VMEM((lines, columns), F32),
+            pltpu.VMEM((2, lines, columns), F32),
             pltpu.VMEM((2, lines, columns), F32),
             pltpu.VMEM((groups, kept + SLABS * LINES, columns // 2), BF16),
             pltpu.VMEM((groups, kept + SLABS * LINES, columns // 2), BF16),
             pltpu.VMEM((lines, channels, double + SLABS * LINES), BF16),
             pltpu.VMEM((lines, channels, double), F32),
             pltpu.VMEM((4, lines, double), F32),
-            pltpu.VMEM((2 * lines, columns), BF16),
-            pltpu.VMEM((2 * lines, columns), BF16),
+            pltpu.VMEM((2, 2 * lines, columns), BF16),
+            pltpu.VMEM((2, 2 * lines, columns), BF16),
             pltpu.VMEM((row_count, 8, double), F32),
             pltpu.VMEM((row_count, 8, double), F32),
             pltpu.VMEM((row_count, 8, double), F32),
@@ -880,11 +890,11 @@
     return pl.pallas_call(
         deliver,
         out_shape=(field, field),
-        in_specs=[hbm] * 2,
+        in_specs=[vmem] * 2,
         out_specs=[hbm] * 2,
-        scratch_shapes=[pltpu.VMEM((4, lines, columns), F32), dma((2, 4))],
+        scratch_shapes=[dma((2,))],
         name="deliver",
-    )(*results)
+    )(*[pltpu.with_memory_space_constraint(x, pltpu.VMEM) for x in results])
 
 
 def solution(mesh):

time: 76.6 us -> 73.4 us (0.958)
  Pallas kernels: 75.7 us -> 72.5 us
    pallas_call x1, Pallas kernels: 73.7 us -> 71.5 us  [shards(): pl.pallas_call(functools.partial(kernel, row_count, col_count, kept), out...]
    pallas_call x1, Pallas kernels: 1.98 us -> 0.99 us  [shards(): pl.pallas_call(deliver, out_shape=(field, field), in_specs=[vmem] * 2, ou...]
where the time goes in v5:
time: 73.4 us; the launch traced here: 73.3 us
  Pallas kernels  72.5 us (99%)
  between operations  0.8 us (1%)
    pallas_call x1, Pallas kernels, shards(): pl.pallas_call(functools.partial(kernel, row_count, col_count, kept), out...  71.5 us

profile of v5, /device:TPU:1, one launch (start us, length us, event | category | flops | bytes accessed | tf_op | source)
XLA Modules:
  0.0 73.3 jit_solution(7522436208299095523)
XLA Ops:
  0.6 71.5 %krylov.1 = (f32[2,64,1024]{2,1,0:T(8,128)S(1)}, f32[2,64,1024]{2,1,0:T(8,128)S(1)}) custom-call(f32[2,64,1024]{2,1,0:T(8,128)} %forcing.1, s32[64,1024]{1,0:T(8,128)} %medium.1, s32[64,1024]{1,0:T(8,128)} %mask.1, s32[16]{0:T(128)} %source_rows.1, s32[16]{0:T(128)} %source_cols.1, f32[8]{0:T(128)} %refraction.1, f32[4,64]{1,0:T(4,128)} %lift_weight.1, ...), custom_call_target="tpu_custom_call" | custom-call | tf_op jit(solution)/shard_map/krylov/pallas_call | solution.py:826
  72.2 1.0 %deliver.1 = (f32[2,64,1024]{2,1,0:T(8,128)}, f32[2,64,1024]{2,1,0:T(8,128)}) custom-call(f32[2,64,1024]{2,1,0:T(8,128)S(1)} %get-tuple-element.4.solution_in, f32[2,64,1024]{2,1,0:T(8,128)S(1)} %get-tuple-element.5.residual_in), custom_call_target="tpu_custom_call" | custom-call | tf_op jit(solution)/shard_map/deliver/pallas_call | solution.py:890

commit v6 on v5

--- a/solution.py
+++ b/solution.py
@@ -39,7 +39,7 @@
     odd = 2 * np.arange(tile_cols // 2, dtype=np.int64) + 1
     mode_index = np.arange(kept_modes, dtype=np.int64)
     angles = (mode_index[:, None] * odd[None, :] % (2 * grid_cols)) * (math.pi / grid_cols)
-    scale = 1.0 / math.sqrt(grid_cols)
+    scale = math.sqrt(0.5 / grid_cols)
     table = np.stack([np.cos(angles), -np.sin(angles)]) * scale
     return table.astype(np.float32).astype(ml_dtypes.bfloat16)
 
@@ -66,8 +66,8 @@
     return high, low, (x - high.astype(F32) - low.astype(F32)).astype(BF16)
 
 
-def gelu(x):
-    return 0.5 * x * (1.0 + lax.erf(x * math.sqrt(0.5)))
+def scaled_gelu(z):
+    return z + z * lax.erf(z)
 
 
 def cmul(a, b):
@@ -152,6 +152,7 @@
     ext,
     applied,
     basis,
+    half_ref,
     table_sems,
     halo_send,
     halo_recv,
@@ -264,12 +265,22 @@
         even_cols[g, kept + LINES * j : kept + LINES * (j + 1), :] = even
         odd_cols[g, LINES * j : LINES * (j + 1), :] = odd
 
-    def field_slabs(g, j, value):
+    def halves(value):
         right, left = value[:, half:], reversed_lanes(value[:, :half])
-        even, odd = split(0.5 * (right + left)), split(0.5 * (right - left))
+        return 0.5 * (right + left), 0.5 * (right - left)
+
+    def field_slabs(g, j, even, odd):
+        even, odd = split(even), split(odd)
         slab(g, j, even[0], odd[0])
         slab(g, j + 1, even[1], odd[1])
         slab(g, j + 2, even[0], odd[0])
+
+    def keep_halves(which, source):
+        for g in range(groups):
+            for p in range(2):
+                even, odd = halves(source[p, rows_of(g), :])
+                half_ref[which, 0, p, rows_of(g), :] = even
+                half_ref[which, 1, p, rows_of(g), :] = odd
 
     def rows_of(g):
         return slice(LINES * g, LINES * (g + 1))
@@ -464,7 +475,6 @@
         ends = [(g, n) for g in sorted({0, groups - 1}) for n in range(outer)]
         inside = [(g, n) for g in range(1, groups - 1) for n in range(outer)]
         order = edges + ends + inside
-        copies = halo_copies(step)
 
         def multiply(g, n, slot):
             left = mixed[LINES * g : LINES * (g + 1)].reshape(LINES * channels, double + wide)
@@ -480,8 +490,9 @@
             lines_of = slice(8 + LINES * g, 8 + LINES * (g + 1))
             even, odd = before[slot, 0], before[slot, 1]
             for side in range(2):
-                active = gelu(even + odd if side else even - odd).astype(BF16)
+                active = scaled_gelu(even + odd if side else even - odd).astype(BF16)
                 out = jnp.dot(project_map[...], active, preferred_element_type=F32)
+                out = out * math.sqrt(0.5)
                 if side:
                     first = 128 + half + PIECE * n
                 else:
@@ -501,17 +512,17 @@
             if t > 0:
                 finish(*order[t - 1], (t - 1) % 2)
             if t == len(edges):
-                for i in (0, 1, 4, 5, 6, 7):
-                    copies[i].start()
+                for copy in halo_copies(step, (0, 1, 4, 5, 6, 7)):
+                    copy.start()
             if t == len(edges) + len(ends):
-                for i in (2, 3):
-                    copies[i].start()
-
-    def halo_copies(step):
+                for copy in halo_copies(step, (2, 3)):
+                    copy.start()
+
+    def halo_copies(step, wanted):
         tall, across_all = pl.ds(8, lines), pl.ds(128, columns)
         line_ends = {
-            1: (pl.ds(lines, 8), pl.ds(0, 8)),
-            -1: (pl.ds(8, 8), pl.ds(8 + lines, 8)),
+            1: (pl.ds(7 + lines, 1), pl.ds(7, 1)),
+            -1: (pl.ds(8, 1), pl.ds(8 + lines, 1)),
             0: (tall, tall),
         }
         col_ends = {
@@ -523,6 +534,8 @@
         for i, (dr, dc) in enumerate(
             [(1, 0), (-1, 0), (0, 1), (0, -1), (1, 1), (1, -1), (-1, 1), (-1, -1)]
         ):
+            if i not in wanted:
+                continue
             here_l, there_l = line_ends[dc]
             here_c, there_c = col_ends[dr]
             copies.append(
@@ -540,8 +553,8 @@
             )
         return copies
 
-    def halos(step):
-        for copy in halo_copies(step):
+    def side_halos(step):
+        for copy in halo_copies(step, (0, 1, 4, 5, 6, 7)):
             copy.wait()
         view = ext.at[step]
 
@@ -553,6 +566,11 @@
         def _():
             view[:, :, 128 + columns :] = jnp.zeros((2, lines + 16, 128), F32)
 
+    def line_halos(step):
+        for copy in halo_copies(step, (2, 3)):
+            copy.wait()
+        view = ext.at[step]
+
         @pl.when(col == 0)
         def _():
             view[:, 0:8, :] = jnp.zeros((2, 8, columns + 256), F32)
@@ -560,6 +578,14 @@
         @pl.when(col == col_count - 1)
         def _():
             view[:, 8 + lines :, :] = jnp.zeros((2, 8, columns + 256), F32)
+
+    def operated(step, each):
+        side_halos(step)
+        for g in range(1, groups - 1):
+            each(g)
+        line_halos(step)
+        for g in sorted({0, groups - 1}):
+            each(g)
 
     def operate(step, g):
         laps, fields = [], []
@@ -602,7 +628,7 @@
     for part in lift_parts:
         point = point + jnp.dot(part, point_weight[...], preferred_element_type=F32)
     channel_row = lax.broadcasted_iota(jnp.int32, (8, channels), 0)
-    point = point + jnp.where(channel_row == 4, layer_bias[...], 0.0)
+    point = (point + jnp.where(channel_row == 4, layer_bias[...], 0.0)) * math.sqrt(0.5)
     top, rest = split(point)
     from_row = lax.broadcasted_iota(jnp.int32, (8, wide), 0)
     slab_of = lax.broadcasted_iota(jnp.int32, (8, wide), 1) // LINES
@@ -647,7 +673,8 @@
         slab(g, 14, zeros, zeros)
         slab(g, 15, zeros, zeros)
         for i in range(2):
-            field_slabs(g, 6 + 3 * i, feature_ref[i, rows_of(g), :])
+            field_slabs(g, 6 + 3 * i, *halves(feature_ref[i, rows_of(g), :]))
+    keep_halves(0, right_ref)
 
     arrived(all_feat, 1, row_count, recv_sems)
     re, im = unrotated(all_feat[...].reshape(2 * lines, double))
@@ -668,11 +695,14 @@
         modes[p, :, kept:] = im[p * lines : (p + 1) * lines] * (grid_scale * inverse_beta)
     for g in range(groups):
         for p in range(2):
-            field_slabs(g, 3 * p, right_ref[p, rows_of(g), :] * (grid_scale * inverse_beta))
+            even, odd = (
+                half_ref[0, i, p, rows_of(g), :] * (grid_scale * inverse_beta) for i in range(2)
+            )
+            field_slabs(g, 3 * p, even, odd)
     layer(0)
-    halos(0)
     sums = [jnp.zeros((8, 128), F32)] * 3
-    for g in range(groups):
+
+    def first_applied(g):
         lines_of = rows_of(g)
         result = operate(0, g)
         for p in range(2):
@@ -682,8 +712,11 @@
             low[1, p * lines + LINES * g : p * lines + LINES * (g + 1), :] = rest
         start = (right_ref[0, lines_of, :], right_ref[1, lines_of, :])
         square = folded(result[0] * result[0] + result[1] * result[1])
-        sums = add(sums, (*pair(start, result), square))
+        sums[:] = add(sums, (*pair(start, result), square))
+
+    operated(0, first_applied)
     send_modes(1, scalar_tile(sums))
+    keep_halves(1, applied.at[0])
     wave_reduce(1)
     arrived(all_wave.at[1], 6, row_count, recv_sems)
     totals = col_total(1)
@@ -713,11 +746,19 @@
         )
         for p in range(2):
             basis[p, lines_of, :] = vector[p]
-            field_slabs(g, 3 * p, vector[p] * grid_scale)
+        even, odd = (
+            next_vector(
+                [half_ref[1, i, p, lines_of, :] for p in range(2)],
+                [half_ref[0, i, p, lines_of, :] for p in range(2)],
+            )
+            for i in range(2)
+        )
+        for p in range(2):
+            field_slabs(g, 3 * p, even[p] * grid_scale, odd[p] * grid_scale)
     layer(1)
-    halos(1)
     sums = [jnp.zeros((8, 128), F32)] * 5
-    for g in range(groups):
+
+    def second_applied(g):
         lines_of = rows_of(g)
         result = operate(1, g)
         for p in range(2):
@@ -725,7 +766,9 @@
         start = (right_ref[0, lines_of, :], right_ref[1, lines_of, :])
         vector = (basis[0, lines_of, :], basis[1, lines_of, :])
         square = folded(result[0] * result[0] + result[1] * result[1])
-        sums = add(sums, (*pair(start, result), *pair(vector, result), square))
+        sums[:] = add(sums, (*pair(start, result), *pair(vector, result), square))
+
+    operated(1, second_applied)
     got_scal[row] = scalar_tile(sums)
     spread(lambda there: got_scal.at[row], got_scal, 8, "row", row, row_count)
     arrived(got_scal, 8, row_count, recv_sems)
@@ -857,6 +900,7 @@
             pltpu.VMEM((2, 2, lines + 16, columns + 256), F32),
             pltpu.VMEM((2, 2, lines, columns), F32),
             pltpu.VMEM((2, lines, columns), F32),
+            pltpu.VMEM((2, 2, 2, lines, columns // 2), F32),
             dma((4 + 2 * groups,)),
             dma((2, 8)),
             dma((2, 8)),

time: 73.4 us -> 72.6 us (0.989)
  Pallas kernels: 72.5 us -> 71.7 us
    pallas_call x1, Pallas kernels: 71.5 us -> 70.7 us  [shards(): pl.pallas_call(functools.partial(kernel, row_count, col_count, kept), out...]
where the time goes in v6:
time: 72.6 us; the launch traced here: 72.5 us
  Pallas kernels  71.7 us (99%)
  between operations  0.8 us (1%)
    pallas_call x1, Pallas kernels, shards(): pl.pallas_call(functools.partial(kernel, row_count, col_count, kept), out...  70.7 us

profile of v6, /device:TPU:1, one launch (start us, length us, event | category | flops | bytes accessed | tf_op | source)
XLA Modules:
  0.0 72.5 jit_solution(2500409403151420925)
XLA Ops:
  0.6 70.7 %krylov.1 = (f32[2,64,1024]{2,1,0:T(8,128)S(1)}, f32[2,64,1024]{2,1,0:T(8,128)S(1)}) custom-call(f32[2,64,1024]{2,1,0:T(8,128)} %forcing.1, s32[64,1024]{1,0:T(8,128)} %medium.1, s32[64,1024]{1,0:T(8,128)} %mask.1, s32[16]{0:T(128)} %source_rows.1, s32[16]{0:T(128)} %source_cols.1, f32[8]{0:T(128)} %refraction.1, f32[4,64]{1,0:T(4,128)} %lift_weight.1, ...), custom_call_target="tpu_custom_call" | custom-call | tf_op jit(solution)/shard_map/krylov/pallas_call | solution.py:869
  71.3 1.0 %deliver.1 = (f32[2,64,1024]{2,1,0:T(8,128)}, f32[2,64,1024]{2,1,0:T(8,128)}) custom-call(f32[2,64,1024]{2,1,0:T(8,128)S(1)} %get-tuple-element.4.solution_in, f32[2,64,1024]{2,1,0:T(8,128)S(1)} %get-tuple-element.5.residual_in), custom_call_target="tpu_custom_call" | custom-call | tf_op jit(solution)/shard_map/deliver/pallas_call | solution.py:934

commit v7 on v6

--- a/solution.py
+++ b/solution.py
@@ -100,13 +100,32 @@
     return y0, y1
 
 
+def far_first(axis, me, count):
+    inner = 2 if axis == "col" else 4
+    if count % inner or count == inner:
+        return [lax.rem(me + d, count) for d in range(1, count)]
+    outer = count // inner
+
+    def hops(step):
+        a, b = step
+        along = min(b, inner - b) if axis == "row" else 0.5 * b
+        return min(a, outer - a) + along
+
+    steps = [(a, b) for a in range(outer) for b in range(inner) if a or b]
+    steps.sort(key=hops, reverse=True)
+    return [
+        lax.rem(me // inner + a, outer) * inner + lax.rem(lax.rem(me, inner) + b, inner)
+        for a, b in steps
+    ]
+
+
 def kernel(
     row_count,
     col_count,
     kept,
-    forcing,
-    medium,
-    mask,
+    forcing_in,
+    medium_in,
+    mask_in,
     source_rows,
     source_cols,
     refraction,
@@ -124,6 +143,9 @@
     phases,
     solution_ref,
     residual_ref,
+    forcing,
+    medium,
+    mask,
     fwd_high,
     fwd_low,
     phase,
@@ -169,6 +191,12 @@
     col = lax.axis_index("col")
     grid_scale = math.sqrt(lines * col_count * columns * row_count)
 
+    first_load = 4 + 2 * groups
+    media_copies = [
+        pltpu.make_async_copy(medium_in, medium, table_sems.at[first_load]),
+        pltpu.make_async_copy(mask_in, mask, table_sems.at[first_load + 1]),
+    ]
+    forcing_copy = pltpu.make_async_copy(forcing_in, forcing, table_sems.at[first_load + 2])
     table_copies = [
         pltpu.make_async_copy(table_high, fwd_high, table_sems.at[0]),
         pltpu.make_async_copy(table_low, fwd_low, table_sems.at[1]),
@@ -183,7 +211,7 @@
         )
     ]
     weight_copy = pltpu.make_async_copy(spectral_weight, weights, table_sems.at[3])
-    for copy in [*table_copies, weight_copy, *back_copies]:
+    for copy in [*media_copies, *table_copies, forcing_copy, weight_copy, *back_copies]:
         copy.start()
 
     barrier = pltpu.get_barrier_semaphore()
@@ -212,8 +240,7 @@
             greeted += 1
 
     def spread(source, target, index, axis, me, count):
-        for d in range(1, count):
-            there = lax.rem(me + d, count)
+        for there in far_first(axis, me, count):
             pltpu.make_async_remote_copy(
                 src_ref=source(there),
                 dst_ref=target.at[me],
@@ -299,6 +326,8 @@
             tile = jnp.where(place == i, jnp.sum(part, axis=0, keepdims=True), tile)
         return tile
 
+    for copy in media_copies:
+        copy.wait()
     for g in range(groups):
         lines_of = rows_of(g)
         kind = medium[lines_of, :]
@@ -339,6 +368,7 @@
     ).astype(BF16)
     source_count = jnp.dot(line_hits, col_hits, preferred_element_type=F32)
     square = jnp.zeros((8, 128), F32)
+    forcing_copy.wait()
     for g in range(groups):
         lines_of = rows_of(g)
         for p in range(2):
@@ -464,34 +494,51 @@
 
                 lax.fori_loop(0, lines // 8, eight_lines, 0)
 
-    def mix_group(g):
+    def mix_part(first, count):
         for kc in range(kept // 128):
             for ob in range(channels // 16):
-                mix_lines(LINES * g, LINES, kc, ob, (0, 1), False, fixed, mixed)
+                mix_lines(first, count, kc, ob, (0, 1), False, fixed, mixed)
 
     def layer(step):
         outer = half // PIECE - 1
-        edges = [(g, outer) for g in range(groups)]
-        ends = [(g, n) for g in sorted({0, groups - 1}) for n in range(outer)]
-        inside = [(g, n) for g in range(1, groups - 1) for n in range(outer)]
+        edges = [(0, outer, 0), (0, outer, 1)] + [(g, outer, None) for g in range(1, groups)]
+        ends = [(g, n, None) for g in sorted({0, groups - 1}) for n in range(outer)]
+        inside = [(g, n, None) for g in range(1, groups - 1) for n in range(outer)]
+        if inside:
+            g, n, _ = inside.pop()
+            inside += [(g, n, 0), (g, n, 1)]
         order = edges + ends + inside
-
-        def multiply(g, n, slot):
-            left = mixed[LINES * g : LINES * (g + 1)].reshape(LINES * channels, double + wide)
+        departures = {edges[-1 - groups // 2]: (0, 1), edges[-1]: range(2, 8), ends[-1]: (8, 9)}
+
+        def place_of(part):
+            return (0, LINES) if part is None else (LINES // 2 * part, LINES // 2)
+
+        def multiply(g, n, part, slot):
+            offset, count = place_of(part)
+            first = LINES * g + offset
+            rows = channels * count
+            left = mixed[first : first + count].reshape(rows, double + wide)
             piece = slice(PIECE * n, PIECE * (n + 1))
-            before[slot, 0] = jnp.dot(
+            before[slot, 0, :rows] = jnp.dot(
                 left[:, : kept + wide], even_cols[g, :, piece], preferred_element_type=F32
             )
-            before[slot, 1] = jnp.dot(
+            before[slot, 1, :rows] = jnp.dot(
                 left[:, kept:], odd_cols[g, :, piece], preferred_element_type=F32
             )
 
-        def finish(g, n, slot):
-            lines_of = slice(8 + LINES * g, 8 + LINES * (g + 1))
-            even, odd = before[slot, 0], before[slot, 1]
+        def finish(g, n, part, slot):
+            offset, count = place_of(part)
+            first_line = 8 + LINES * g + offset
+            lines_of = slice(first_line, first_line + count)
+            rows = channels * count
+            project = project_map[:, channels * offset : channels * offset + rows]
+            even, odd = before[slot, 0, :rows], before[slot, 1, :rows]
             for side in range(2):
                 active = scaled_gelu(even + odd if side else even - odd).astype(BF16)
-                out = jnp.dot(project_map[...], active, preferred_element_type=F32)
+                out = jnp.dot(project, active, preferred_element_type=F32)
+                out = jnp.concatenate(
+                    [out[LINES * p + offset : LINES * p + offset + count] for p in range(2)], axis=0
+                )
                 out = out * math.sqrt(0.5)
                 if side:
                     first = 128 + half + PIECE * n
@@ -499,23 +546,20 @@
                     first = 128 + half - PIECE * (n + 1)
                     out = reversed_lanes(out)
                 place = slice(first, first + PIECE)
-                ext[step, 0, lines_of, place] = out[:LINES]
-                ext[step, 1, lines_of, place] = out[LINES:]
-
-        mix_group(0)
+                ext[step, 0, lines_of, place] = out[:count]
+                ext[step, 1, lines_of, place] = out[count:]
+
+        mix_part(0, LINES // 2)
         for t in range(len(order) + 1):
             if t < len(order):
-                g, n = order[t]
-                multiply(g, n, t % 2)
-                if t < len(edges) and g + 1 < groups:
-                    mix_group(g + 1)
+                multiply(*order[t], t % 2)
+                if t == 0:
+                    mix_part(LINES // 2, LINES // 2)
+                elif t < groups:
+                    mix_part(LINES * t, LINES)
             if t > 0:
                 finish(*order[t - 1], (t - 1) % 2)
-            if t == len(edges):
-                for copy in halo_copies(step, (0, 1, 4, 5, 6, 7)):
-                    copy.start()
-            if t == len(edges) + len(ends):
-                for copy in halo_copies(step, (2, 3)):
+                for copy in halo_copies(step, departures.get(order[t - 1], ())):
                     copy.start()
 
     def halo_copies(step, wanted):
@@ -531,12 +575,12 @@
             0: (across_all, across_all),
         }
         copies = []
-        for i, (dr, dc) in enumerate(
-            [(1, 0), (-1, 0), (0, 1), (0, -1), (1, 1), (1, -1), (-1, 1), (-1, -1)]
-        ):
-            if i not in wanted:
-                continue
+        moves = [(1, 0), (-1, 0), (1, 0), (-1, 0), (1, 1), (1, -1), (-1, 1), (-1, -1), (0, 1), (0, -1)]
+        for i in wanted:
+            dr, dc = moves[i]
             here_l, there_l = line_ends[dc]
+            if i < 4:
+                here_l = there_l = pl.ds(8 + (i // 2) * (lines // 2), lines // 2)
             here_c, there_c = col_ends[dr]
             copies.append(
                 pltpu.make_async_remote_copy(
@@ -554,7 +598,7 @@
         return copies
 
     def side_halos(step):
-        for copy in halo_copies(step, (0, 1, 4, 5, 6, 7)):
+        for copy in halo_copies(step, range(8)):
             copy.wait()
         view = ext.at[step]
 
@@ -567,7 +611,7 @@
             view[:, :, 128 + columns :] = jnp.zeros((2, lines + 16, 128), F32)
 
     def line_halos(step):
-        for copy in halo_copies(step, (2, 3)):
+        for copy in halo_copies(step, (8, 9)):
             copy.wait()
         view = ext.at[step]
 
@@ -685,20 +729,20 @@
     for copy in back_copies:
         copy.wait()
 
-    arrived(all_wave.at[0], 3, row_count, recv_sems)
     total_square = col_total(0)[0:1, :]
     beta = jnp.sqrt(total_square + norm_eps)
     inverse_beta = 1.0 / beta
-    re, im = unrotated(all_wave[0].reshape(2 * lines, double))
-    for p in range(2):
-        modes[p, :, :kept] = re[p * lines : (p + 1) * lines] * (grid_scale * inverse_beta)
-        modes[p, :, kept:] = im[p * lines : (p + 1) * lines] * (grid_scale * inverse_beta)
     for g in range(groups):
         for p in range(2):
             even, odd = (
                 half_ref[0, i, p, rows_of(g), :] * (grid_scale * inverse_beta) for i in range(2)
             )
             field_slabs(g, 3 * p, even, odd)
+    arrived(all_wave.at[0], 3, row_count, recv_sems)
+    re, im = unrotated(all_wave[0].reshape(2 * lines, double))
+    for p in range(2):
+        modes[p, :, :kept] = re[p * lines : (p + 1) * lines] * (grid_scale * inverse_beta)
+        modes[p, :, kept:] = im[p * lines : (p + 1) * lines] * (grid_scale * inverse_beta)
     layer(0)
     sums = [jnp.zeros((8, 128), F32)] * 3
 
@@ -718,7 +762,6 @@
     send_modes(1, scalar_tile(sums))
     keep_halves(1, applied.at[0])
     wave_reduce(1)
-    arrived(all_wave.at[1], 6, row_count, recv_sems)
     totals = col_total(1)
     unit_square = total_square * inverse_beta * inverse_beta
     a = (totals[0:1, :] * inverse_beta, totals[1:2, :] * inverse_beta)
@@ -732,12 +775,6 @@
         scaled = cmul(a_over, v)
         return (w[0] - scaled[0]) * inverse_c, (w[1] - scaled[1]) * inverse_c
 
-    old, new = (all_wave[i].reshape(2 * lines, double) for i in range(2))
-    planes = next_vector((new[:lines], new[lines:]), (old[:lines], old[lines:]))
-    for p in range(2):
-        re, im = unrotated(planes[p])
-        modes[p, :, :kept] = re * grid_scale
-        modes[p, :, kept:] = im * grid_scale
     for g in range(groups):
         lines_of = rows_of(g)
         vector = next_vector(
@@ -755,6 +792,13 @@
         )
         for p in range(2):
             field_slabs(g, 3 * p, even[p] * grid_scale, odd[p] * grid_scale)
+    arrived(all_wave.at[1], 6, row_count, recv_sems)
+    old, new = (all_wave[i].reshape(2 * lines, double) for i in range(2))
+    planes = next_vector((new[:lines], new[lines:]), (old[:lines], old[lines:]))
+    for p in range(2):
+        re, im = unrotated(planes[p])
+        modes[p, :, :kept] = re * grid_scale
+        modes[p, :, kept:] = im * grid_scale
     layer(1)
     sums = [jnp.zeros((8, 128), F32)] * 5
 
@@ -869,9 +913,12 @@
     results = pl.pallas_call(
         functools.partial(kernel, row_count, col_count, kept),
         out_shape=(pltpu.VMEM(field.shape, F32), pltpu.VMEM(field.shape, F32)),
-        in_specs=[vmem] * 3 + [smem] * 5 + [vmem] * 2 + [hbm] + [vmem] * 3 + [hbm] * 4,
+        in_specs=[hbm] * 3 + [smem] * 5 + [vmem] * 2 + [hbm] + [vmem] * 3 + [hbm] * 4,
         out_specs=(vmem, vmem),
         scratch_shapes=[
+            pltpu.VMEM((2, lines, columns), F32),
+            pltpu.VMEM((lines, columns), jnp.int32),
+            pltpu.VMEM((lines, columns), jnp.int32),
             pltpu.VMEM((columns, double), BF16),
             pltpu.VMEM((columns, double), BF16),
             pltpu.VMEM((8, 2 * double), F32),
@@ -901,9 +948,9 @@
             pltpu.VMEM((2, 2, lines, columns), F32),
             pltpu.VMEM((2, lines, columns), F32),
             pltpu.VMEM((2, 2, 2, lines, columns // 2), F32),
-            dma((4 + 2 * groups,)),
-            dma((2, 8)),
-            dma((2, 8)),
+            dma((7 + 2 * groups,)),
+            dma((2, 10)),
+            dma((2, 10)),
             dma((10,)),
             dma((10,)),
         ],

time: 72.6 us -> 70.5 us (0.971)
  Pallas kernels: 71.7 us -> 69.5 us
    pallas_call x1, Pallas kernels: 70.7 us -> 68.5 us  [shards(): pl.pallas_call(functools.partial(kernel, row_count, col_count, kept), out...]
where the time goes in v7:
time: 70.5 us; the launch traced here: 70.3 us
  Pallas kernels  69.5 us (99%)
  between operations  0.8 us (1%)
    pallas_call x1, Pallas kernels, shards(): pl.pallas_call(functools.partial(kernel, row_count, col_count, kept), out...  68.5 us

profile of v7, /device:TPU:1, one launch (start us, length us, event | category | flops | bytes accessed | tf_op | source)
XLA Modules:
  0.0 70.3 jit_solution(18263443992114677422)
XLA Ops:
  0.6 68.5 %krylov.1 = (f32[2,64,1024]{2,1,0:T(8,128)S(1)}, f32[2,64,1024]{2,1,0:T(8,128)S(1)}) custom-call(f32[2,64,1024]{2,1,0:T(8,128)} %forcing_in.1, s32[64,1024]{1,0:T(8,128)} %medium_in.1, s32[64,1024]{1,0:T(8,128)} %mask_in.1, s32[16]{0:T(128)} %source_rows.1, s32[16]{0:T(128)} %source_cols.1, f32[8]{0:T(128)} %refraction.1, f32[4,64]{1,0:T(4,128)} %lift_weight.1, ...), custom_call_target="tpu_custom_call" | custom-call | tf_op jit(solution)/shard_map/krylov/pallas_call | solution.py:913
  69.2 1.0 %deliver.1 = (f32[2,64,1024]{2,1,0:T(8,128)}, f32[2,64,1024]{2,1,0:T(8,128)}) custom-call(f32[2,64,1024]{2,1,0:T(8,128)S(1)} %get-tuple-element.4.solution_in, f32[2,64,1024]{2,1,0:T(8,128)S(1)} %get-tuple-element.5.residual_in), custom_call_target="tpu_custom_call" | custom-call | tf_op jit(solution)/shard_map/deliver/pallas_call | solution.py:981

commit v8 on v7

--- a/solution.py
+++ b/solution.py
@@ -494,51 +494,34 @@
 
                 lax.fori_loop(0, lines // 8, eight_lines, 0)
 
-    def mix_part(first, count):
+    def mix_group(g):
         for kc in range(kept // 128):
             for ob in range(channels // 16):
-                mix_lines(first, count, kc, ob, (0, 1), False, fixed, mixed)
+                mix_lines(LINES * g, LINES, kc, ob, (0, 1), False, fixed, mixed)
 
     def layer(step):
         outer = half // PIECE - 1
-        edges = [(0, outer, 0), (0, outer, 1)] + [(g, outer, None) for g in range(1, groups)]
-        ends = [(g, n, None) for g in sorted({0, groups - 1}) for n in range(outer)]
-        inside = [(g, n, None) for g in range(1, groups - 1) for n in range(outer)]
-        if inside:
-            g, n, _ = inside.pop()
-            inside += [(g, n, 0), (g, n, 1)]
+        edges = [(g, outer) for g in range(groups)]
+        ends = [(g, n) for g in sorted({0, groups - 1}) for n in range(outer)]
+        inside = [(g, n) for g in range(1, groups - 1) for n in range(outer)]
         order = edges + ends + inside
-        departures = {edges[-1 - groups // 2]: (0, 1), edges[-1]: range(2, 8), ends[-1]: (8, 9)}
-
-        def place_of(part):
-            return (0, LINES) if part is None else (LINES // 2 * part, LINES // 2)
-
-        def multiply(g, n, part, slot):
-            offset, count = place_of(part)
-            first = LINES * g + offset
-            rows = channels * count
-            left = mixed[first : first + count].reshape(rows, double + wide)
+
+        def multiply(g, n, slot):
+            left = mixed[LINES * g : LINES * (g + 1)].reshape(LINES * channels, double + wide)
             piece = slice(PIECE * n, PIECE * (n + 1))
-            before[slot, 0, :rows] = jnp.dot(
+            before[slot, 0] = jnp.dot(
                 left[:, : kept + wide], even_cols[g, :, piece], preferred_element_type=F32
             )
-            before[slot, 1, :rows] = jnp.dot(
+            before[slot, 1] = jnp.dot(
                 left[:, kept:], odd_cols[g, :, piece], preferred_element_type=F32
             )
 
-        def finish(g, n, part, slot):
-            offset, count = place_of(part)
-            first_line = 8 + LINES * g + offset
-            lines_of = slice(first_line, first_line + count)
-            rows = channels * count
-            project = project_map[:, channels * offset : channels * offset + rows]
-            even, odd = before[slot, 0, :rows], before[slot, 1, :rows]
+        def finish(g, n, slot):
+            lines_of = slice(8 + LINES * g, 8 + LINES * (g + 1))
+            even, odd = before[slot, 0], before[slot, 1]
             for side in range(2):
                 active = scaled_gelu(even + odd if side else even - odd).astype(BF16)
-                out = jnp.dot(project, active, preferred_element_type=F32)
-                out = jnp.concatenate(
-                    [out[LINES * p + offset : LINES * p + offset + count] for p in range(2)], axis=0
-                )
+                out = jnp.dot(project_map[...], active, preferred_element_type=F32)
                 out = out * math.sqrt(0.5)
                 if side:
                     first = 128 + half + PIECE * n
@@ -546,20 +529,26 @@
                     first = 128 + half - PIECE * (n + 1)
                     out = reversed_lanes(out)
                 place = slice(first, first + PIECE)
-                ext[step, 0, lines_of, place] = out[:count]
-                ext[step, 1, lines_of, place] = out[count:]
-
-        mix_part(0, LINES // 2)
+                ext[step, 0, lines_of, place] = out[:LINES]
+                ext[step, 1, lines_of, place] = out[LINES:]
+
+        mix_group(0)
         for t in range(len(order) + 1):
             if t < len(order):
-                multiply(*order[t], t % 2)
-                if t == 0:
-                    mix_part(LINES // 2, LINES // 2)
-                elif t < groups:
-                    mix_part(LINES * t, LINES)
+                g, n = order[t]
+                multiply(g, n, t % 2)
+                if t < len(edges) and g + 1 < groups:
+                    mix_group(g + 1)
             if t > 0:
                 finish(*order[t - 1], (t - 1) % 2)
-                for copy in halo_copies(step, departures.get(order[t - 1], ())):
+            if t == groups // 2:
+                for copy in halo_copies(step, (0, 1)):
+                    copy.start()
+            if t == len(edges):
+                for copy in halo_copies(step, (2, 3, 4, 5, 6, 7)):
+                    copy.start()
+            if t == len(edges) + len(ends):
+                for copy in halo_copies(step, (8, 9)):
                     copy.start()
 
     def halo_copies(step, wanted):

time: 70.5 us -> 70.3 us (level)
  no operation moved by 1% of the time
where the time goes in v8:
time: 70.3 us; the launch traced here: 70.2 us
  Pallas kernels  69.3 us (99%)
  between operations  0.8 us (1%)
    pallas_call x1, Pallas kernels, shards(): pl.pallas_call(functools.partial(kernel, row_count, col_count, kept), out...  68.4 us

profile of v8, /device:TPU:1, one launch (start us, length us, event | category | flops | bytes accessed | tf_op | source)
XLA Modules:
  0.0 70.2 jit_solution(5985076261539645676)
XLA Ops:
  0.6 68.4 %krylov.1 = (f32[2,64,1024]{2,1,0:T(8,128)S(1)}, f32[2,64,1024]{2,1,0:T(8,128)S(1)}) custom-call(f32[2,64,1024]{2,1,0:T(8,128)} %forcing_in.1, s32[64,1024]{1,0:T(8,128)} %medium_in.1, s32[64,1024]{1,0:T(8,128)} %mask_in.1, s32[16]{0:T(128)} %source_rows.1, s32[16]{0:T(128)} %source_cols.1, f32[8]{0:T(128)} %refraction.1, f32[4,64]{1,0:T(4,128)} %lift_weight.1, ...), custom_call_target="tpu_custom_call" | custom-call | tf_op jit(solution)/shard_map/krylov/pallas_call | solution.py:902
  69.0 1.0 %deliver.1 = (f32[2,64,1024]{2,1,0:T(8,128)}, f32[2,64,1024]{2,1,0:T(8,128)}) custom-call(f32[2,64,1024]{2,1,0:T(8,128)S(1)} %get-tuple-element.4.solution_in, f32[2,64,1024]{2,1,0:T(8,128)S(1)} %get-tuple-element.5.residual_in), custom_call_target="tpu_custom_call" | custom-call | tf_op jit(solution)/shard_map/deliver/pallas_call | solution.py:970
